TPU v7x, 32 devices: a whole 2x2x4 slice. The times are simulated.
32 devices in a mesh: dom: 4 (over x, core), sub: 8 (over z, y).
Axes of the slice: x: 2, y: 2, z: 4, core: 2. Of those that a mesh axis runs over, the one named last changes fastest.
Arguments:
- node_feat: bfloat16 [96, 192, 128], P('dom', 'sub'), may hold values from -6 to 6
- edge_feat: bfloat16 [32768, 128], P(('dom', 'sub')), may hold values from -6 to 6
- edge_dst: int32 [32768], P(('dom', 'sub')), may hold values from 0 to 575
- edge_dir: int32 [32768], P(('dom', 'sub')), may hold values from 0 to 3, as said below
- edge_count: int32 [32], P(('dom', 'sub')), may hold values from 512 to 1024, as said below
- w_edge_in: bfloat16 [384, 128], P('dom'), may hold values from -0.3125 to 0.3125
- w_edge_out: bfloat16 [128, 128], P('dom'), may hold values from -0.5 to 0.5
- w_node_in: bfloat16 [256, 128], P('dom'), may hold values from -0.375 to 0.375
- w_node_out: bfloat16 [128, 128], P('dom'), may hold values from -0.5 to 0.5
- gains: bfloat16 [2, 128], P(None, 'dom'), may hold values from 0.099609375 to 1.8984375
- node_cot: bfloat16 [96, 192, 128], P('dom', 'sub'), may hold values from -6 to 6
- edge_cot: bfloat16 [32768, 128], P(('dom', 'sub')), may hold values from -6 to 6
Outputs:
- node_grad: bfloat16 [96, 192, 128], P('dom', 'sub')
- edge_grad: bfloat16 [32768, 128], P(('dom', 'sub'))
- w_edge_in_grad: float32 [384, 128], P('dom')
- w_edge_out_grad: float32 [128, 128], P('dom')
- w_node_in_grad: float32 [256, 128], P('dom')
- w_node_out_grad: float32 [128, 128], P('dom')
- gain_grad: float32 [2, 128], P(None, 'dom')
Inputs may be any that keep to these rules, and one draw needn't show every extreme that they name: `edge_dir`: the sender lies inside the global grid. A device's live edges are its first edge_count slots; some device is full.
All inputs are finite; a program needn't handle non-finite values.
Results may differ from a plain program's by a relative error of at most 0.033.
The roundings to bfloat16 on the way count: a program that leaves them out, or rounds other values in their place, can miss the bound.
Values may be sent and summed in bfloat16 or wider, within the bound.
A program may use at most 64 MiB of HBM per device.

v0:
```python
import jax
import jax.numpy as jnp
from jax import lax
from jax.sharding import PartitionSpec as P


def with_halo(block, sides, width):
    for axis, dim in sides:
        count = lax.axis_size(axis)
        forward = [(i, i + 1) for i in range(count - 1)]
        backward = [(target, source) for source, target in forward]
        low = lax.ppermute(
            lax.slice_in_dim(block, block.shape[dim] - width, None, axis=dim), axis, forward
        )
        high = lax.ppermute(lax.slice_in_dim(block, 0, width, axis=dim), axis, backward)
        block = jnp.concatenate([low, block, high], axis=dim)
    return block


def layer_norm(raw_out):
    average = jnp.mean(raw_out, axis=-1, keepdims=True)
    centered = raw_out - average
    inv_std = lax.rsqrt(jnp.mean(centered * centered, axis=-1, keepdims=True) + 1e-05)
    return (centered * inv_std, inv_std)


def norm_back(upstream, normed, inv_std):
    return (
        upstream
        - jnp.mean(upstream, axis=-1, keepdims=True)
        - normed * jnp.mean(upstream * normed, axis=-1, keepdims=True)
    ) * inv_std


def mlp_forward(inputs, w_first, w_second, gain_vec):
    pre_act = jnp.dot(inputs, w_first, preferred_element_type=jnp.float32)
    hidden = jnp.maximum(pre_act, 0.0).astype(jnp.bfloat16)
    raw_out = jnp.dot(hidden, w_second, preferred_element_type=jnp.float32)
    normed, inv_std = layer_norm(raw_out)
    return (pre_act, hidden, normed, inv_std, normed * gain_vec)


def mlp_backward(upstream, inputs, pre_act, hidden, normed, inv_std, gain_vec, w_first, w_second):
    gain_part = jnp.sum(upstream * normed, axis=0)
    grad_raw = norm_back(upstream * gain_vec, normed, inv_std).astype(jnp.bfloat16)
    second_part = jnp.dot(hidden.T, grad_raw, preferred_element_type=jnp.float32)
    grad_hidden = jnp.dot(grad_raw, w_second.T, preferred_element_type=jnp.float32)
    grad_pre = jnp.where(pre_act > 0, grad_hidden, 0.0).astype(jnp.bfloat16)
    first_part = jnp.dot(inputs.T, grad_pre, preferred_element_type=jnp.float32)
    grad_inputs = jnp.dot(grad_pre, w_first.T, preferred_element_type=jnp.float32)
    return (grad_inputs, first_part, second_part, gain_part)


def shards(
    node_feat,
    edge_feat,
    edge_dst,
    edge_dir,
    edge_count,
    w_edge_in,
    w_edge_out,
    w_node_in,
    w_node_out,
    gains,
    node_cot,
    edge_cot,
):
    full_edge_in, full_edge_out, full_node_in, full_node_out, full_gains = (
        lax.all_gather(w_edge_in, "dom", axis=0, tiled=True),
        lax.all_gather(w_edge_out, "dom", axis=0, tiled=True),
        lax.all_gather(w_node_in, "dom", axis=0, tiled=True),
        lax.all_gather(w_node_out, "dom", axis=0, tiled=True),
        lax.all_gather(gains, "dom", axis=1, tiled=True),
    )
    gain_edge = full_gains[0].astype(jnp.float32)
    gain_node = full_gains[1].astype(jnp.float32)
    block_side = node_feat.shape[0]
    latent = node_feat.shape[2]
    padded_side = block_side + 2
    padded = with_halo(node_feat, (("dom", 0), ("sub", 1)), 1).reshape(
        padded_side * padded_side, latent
    )
    node_row = edge_dst // block_side
    node_col = edge_dst % block_side
    step_row = jnp.where(edge_dir == 0, 1, jnp.where(edge_dir == 1, -1, 0)).astype(jnp.int32)
    step_col = jnp.where(edge_dir == 2, 1, jnp.where(edge_dir == 3, -1, 0)).astype(jnp.int32)
    target_pad = (node_row + 1) * padded_side + node_col + 1
    source_pad = (node_row + 1 + step_row) * padded_side + node_col + 1 + step_col
    active = (jnp.arange(edge_dst.shape[0], dtype=jnp.int32) < edge_count[0]).astype(jnp.float32)[
        :, None
    ]
    inputs = jnp.concatenate([edge_feat, padded[source_pad], padded[target_pad]], axis=1)
    pre_e, hidden_e, normed_e, inv_e, message = mlp_forward(
        inputs, full_edge_in, full_edge_out, gain_edge
    )
    aggregate = jax.ops.segment_sum(
        message * active, edge_dst, num_segments=block_side * block_side
    )
    node_rows = node_feat.reshape(block_side * block_side, latent)
    node_input = jnp.concatenate([node_rows, aggregate.astype(jnp.bfloat16)], axis=1)
    pre_n, hidden_n, normed_n, inv_n, _ = mlp_forward(
        node_input, full_node_in, full_node_out, gain_node
    )
    node_upstream = node_cot.reshape(block_side * block_side, latent).astype(jnp.float32)
    node_in_grad, node_first, node_second, node_gain = mlp_backward(
        node_upstream,
        node_input,
        pre_n,
        hidden_n,
        normed_n,
        inv_n,
        gain_node,
        full_node_in,
        full_node_out,
    )
    cot_float = edge_cot.astype(jnp.float32)
    upstream = active * (cot_float + node_in_grad[:, latent:][edge_dst])
    edge_in_grad, edge_first, edge_second, edge_gain = mlp_backward(
        upstream, inputs, pre_e, hidden_e, normed_e, inv_e, gain_edge, full_edge_in, full_edge_out
    )
    edge_grad = (cot_float + edge_in_grad[:, :latent]).astype(jnp.bfloat16)
    spread = jnp.zeros((padded_side * padded_side, latent), jnp.float32)
    spread = (
        spread.at[source_pad]
        .add(edge_in_grad[:, latent : 2 * latent])
        .at[target_pad]
        .add(edge_in_grad[:, 2 * latent :])
    )
    spread = spread.reshape(padded_side, padded_side, latent)
    outgoing = jnp.stack(
        [
            jnp.stack([spread[1:-1, 0], spread[0, 1:-1]]),
            jnp.stack([spread[-1, 1:-1], spread[1:-1, -1]]),
        ]
    )
    incoming = with_halo(outgoing.astype(jnp.bfloat16), (("dom", 0), ("sub", 1)), 1).astype(
        outgoing.dtype
    )
    inner = spread[1:-1, 1:-1]
    inner = inner.at[0].add(incoming[0, 1]).at[-1].add(incoming[3, 2])
    inner = inner.at[:, 0].add(incoming[2, 0]).at[:, -1].add(incoming[1, 3])
    node_total = node_upstream + node_in_grad[:, :latent]
    node_grad = (node_total.reshape(block_side, block_side, latent) + inner).astype(jnp.bfloat16)
    nodes_all = block_side * block_side * lax.axis_size("dom") * lax.axis_size("sub")
    grad_scale = lax.rsqrt(jnp.float32(nodes_all))
    gain_terms = jnp.stack([edge_gain, node_gain]) * grad_scale
    local_terms = (
        edge_first * grad_scale,
        edge_second * grad_scale,
        node_first * grad_scale,
        node_second * grad_scale,
        gain_terms,
    )
    summed = lax.psum(
        (local_terms[0], local_terms[1], local_terms[2], local_terms[3], local_terms[4]), "sub"
    )
    results = (
        lax.psum_scatter(
            summed[0].astype(jnp.bfloat16), "dom", scatter_dimension=0, tiled=True
        ).astype(jnp.float32),
        lax.psum_scatter(
            summed[1].astype(jnp.bfloat16), "dom", scatter_dimension=0, tiled=True
        ).astype(jnp.float32),
        lax.psum_scatter(
            summed[2].astype(jnp.bfloat16), "dom", scatter_dimension=0, tiled=True
        ).astype(jnp.float32),
        lax.psum_scatter(
            summed[3].astype(jnp.bfloat16), "dom", scatter_dimension=0, tiled=True
        ).astype(jnp.float32),
        lax.psum_scatter(
            summed[4].astype(jnp.bfloat16), "dom", scatter_dimension=1, tiled=True
        ).astype(jnp.float32),
    )
    return (node_grad, edge_grad, results[0], results[1], results[2], results[3], results[4])


def solution(mesh):
    in_specs = (
        P("dom", "sub", None),
        P(("dom", "sub"), None),
        P(("dom", "sub")),
        P(("dom", "sub")),
        P(("dom", "sub")),
        P("dom", None),
        P("dom", None),
        P("dom", None),
        P("dom", None),
        P(None, "dom"),
        P("dom", "sub", None),
        P(("dom", "sub"), None),
    )
    out_specs = (
        P("dom", "sub", None),
        P(("dom", "sub"), None),
        P("dom", None),
        P("dom", None),
        P("dom", None),
        P("dom", None),
        P(None, "dom"),
    )
    return jax.shard_map(shards, mesh=mesh, in_specs=in_specs, out_specs=out_specs, check_vma=False)
```

profile of v0, /device:TPU:0, one launch (start us, length us, event | category | flops | bytes accessed | tf_op | source)
XLA Modules:
  0.0 235.3 jit_solution(5932185349745399566)
XLA Ops:
  7.2 0.8 fusion.33
  8.0 1.3 collective-permute-start.1
  9.3 3.0 %collective-permute-start = (bf16[1,24,128]{2,1,0:T(8,128)(2,1)S(1)}, bf16[1,24,128]{2,1,0:T(8,128)(2,1)S(1)}, u32[]{:S(2)}, u32[]{:S(2)}) collective-permute-start(bf16[1,24,128]{2,1,0:T(8,128)(2,1)S(1)} %get-tuple-element.99), channel_id=1, source_target_pairs={{0,8},{8,16},{16,24},{1,9},{9,17},{17,25},{2,10},{10,18},{18,26},{... | collective-permute-start | bytes 18440 | tf_op jit(solution)/shard_map/ppermute | solution.py:12
  12.3 6.4 %all-gather = bf16[4,32,2]{1,2,0:T(2,128)(2,1)S(1)} all-gather(bf16[1,32,2]{1,2,0:T(2,128)(2,1)} %bitcast.80), channel_id=1, replica_groups=mesh['dom'=4,'sub'=8] {'dom'}, dimensions={0}, use_global_device_ids=true | all-gather | bytes 640 | tf_op jit(solution)/shard_map/all_gather | solution.py:73
  18.8 1.1 fusion.8
  19.9 0.9 bitcast_multiply_fusion.1
  21.5 5.5 %all_gather.18 = bf16[256,128]{1,0:T(8,128)(2,1)S(1)} all-gather(bf16[64,128]{1,0:T(8,128)(2,1)} %param.27), channel_id=1, replica_groups=mesh['dom'=4,'sub'=8] {'dom'}, dimensions={0}, use_global_device_ids=true | all-gather | bytes 81920 | tf_op jit(solution)/shard_map/all_gather | solution.py:71
  27.0 5.5 %all_gather.15 = bf16[384,128]{1,0:T(8,128)(2,1)S(1)} all-gather(bf16[96,128]{1,0:T(8,128)(2,1)} %param.25), channel_id=1, replica_groups=mesh['dom'=4,'sub'=8] {'dom'}, dimensions={0}, use_global_device_ids=true | all-gather | bytes 122880 | tf_op jit(solution)/shard_map/all_gather | solution.py:69
  32.5 1.0 constant_dynamic-update-slice_fusion.5
  33.5 1.3 broadcast_clamp_fusion
  34.8 5.4 %all_gather.16 = bf16[128,128]{1,0:T(8,128)(2,1)S(1)} all-gather(bf16[32,128]{1,0:T(8,128)(2,1)} %param.26), channel_id=1, replica_groups=mesh['dom'=4,'sub'=8] {'dom'}, dimensions={0}, use_global_device_ids=true | all-gather | bytes 40960 | tf_op jit(solution)/shard_map/all_gather | solution.py:70
  40.3 0.1 copy.38
  40.6 3.6 %collective-permute-start.2 = (bf16[26,1,128]{2,1,0:T(2,128)(2,1)S(1)}, bf16[26,1,128]{2,1,0:T(2,128)(2,1)S(1)}, u32[]{:S(2)}, u32[]{:S(2)}) collective-permute-start(bf16[26,1,128]{2,1,0:T(2,128)(2,1)S(1)} %get-tuple-element.96), channel_id=1, source_target_pairs={{0,1},{1,2},{2,3},{3,4},{4,5},{5,6},{6,7},{8,9},{9,10},{10,11},{11... | collective-permute-start | bytes 19976 | tf_op jit(solution)/shard_map/ppermute | solution.py:12
  44.2 1.3 collective-permute-start.3
  45.6 5.2 %all_gather.19 = bf16[128,128]{1,0:T(8,128)(2,1)S(1)} all-gather(bf16[32,128]{1,0:T(8,128)(2,1)S(1)} %copy-done.10), channel_id=1, replica_groups=mesh['dom'=4,'sub'=8] {'dom'}, dimensions={0}, use_global_device_ids=true | all-gather | bytes 40960 | tf_op jit(solution)/shard_map/all_gather | solution.py:72
  50.8 0.1 pad_maximum_fusion.1
  50.9 3.2 %gather_fusion.1 = bf16[1024,128]{1,0:T(8,128)(2,1)S(1)} fusion(bf16[676,128]{1,0:T(8,128)(2,1)S(1)} %reshape.207, s32[1024]{0:T(1024)S(1)} %get-tuple-element.86), kind=kCustom, calls=%fused_computation.1 | custom fusion | bytes 528384 | tf_op jit(solution)/shard_map/gather | solution.py:92
  54.1 3.2 %gather_fusion = bf16[1024,128]{1,0:T(8,128)(2,1)S(1)} fusion(bf16[676,128]{1,0:T(8,128)(2,1)S(1)} %reshape.207, s32[1024]{0:T(1024)S(1)} %get-tuple-element.106), kind=kCustom, calls=%fused_computation | custom fusion | bytes 528384 | tf_op jit(solution)/shard_map/gather | solution.py:92
  57.5 0.4 fusion.37
  57.9 0.3 fusion.35
  58.3 0.1 multiply_multiply_fusion
  58.4 1.0 copy.37
  59.4 6.5 %scatter_custom_fusion = f32[576,128]{1,0:T(8,128)S(1)} fusion(s32[1024]{0:T(1024)} %param.22, f32[1024,128]{1,0:T(8,128)} %copy.37, f32[]{:T(128)} %constant.151.clone.1), kind=kCustom, calls=%fused_computation.47 | custom fusion | flops 131072 | bytes 295424 | tf_op jit(solution)/shard_map/scatter-add | solution.py:96
  65.9 0.2 fusion.11
  66.1 0.3 fusion.36
  66.5 0.3 multiply_reduce_fusion.5
  66.8 0.8 fusion.9
  67.5 0.4 multiply_convert_fusion.1
  67.9 0.9 convolution_multiply_fusion.2
  68.8 0.2 fusion.1
  69.0 1.0 convolution_multiply_fusion.1
  69.9 0.2 fusion.38
  70.2 0.8 slice_add_fusion
  70.9 2.8 %gather_fusion.2 = f32[1024,128]{1,0:T(8,128)S(1)} fusion(f32[576,128]{1,0:T(8,128)S(1)} %get-tuple-element.91, s32[1024]{0:T(1024)S(1)} %get-tuple-element.105), kind=kCustom, calls=%fused_computation.2 | custom fusion | bytes 1052672 | tf_op jit(solution)/shard_map/gather | solution.py:117
  73.7 0.2 copy.39
  74.0 0.9 multiply_reduce_fusion
  74.9 0.2 multiply_convert_fusion
  75.1 0.3 convolution_multiply_fusion.3
  75.4 0.3 fusion
  75.7 0.4 convolution_multiply_fusion
  76.1 0.4 fusion.39
  76.6 44.8 %all-reduce.2 = (bf16[384,128]{1,0:T(8,128)(2,1)}, bf16[128,128]{1,0:T(8,128)(2,1)}, bf16[256,128]{1,0:T(8,128)(2,1)}, bf16[128,128]{1,0:T(8,128)(2,1)}, bf16[2,128]{1,0:T(2,128)(2,1)S(1)}) all-reduce(f32[384,128]{1,0:T(8,128)S(1)} %convolution_multiply_fusion, ...), channel_id=1, replica_groups=mesh['dom'=4,'sub'=8] {'sub'}, use_global_device_ids=true, to_apply=%region_11.12 | all-reduce | flops 114944 | bytes 689664 | tf_op jit(solution)/shard_map/psum | solution.py:154
  121.4 0.7 copy.46
  122.2 6.3 %scatter_custom_fusion.1 = f32[676,128]{1,0:T(8,128)S(1)} fusion(s32[1024]{0:T(1024)} %get-tuple-element.107, f32[1024,384]{1,0:T(8,128)S(1)} %fusion.39, f32[]{:T(128)} %constant.151.clone.1), kind=kCustom, calls=%fused_computation.20 | custom fusion | flops 131072 | bytes 870912 | tf_op jit(solution)/shard_map/scatter-add | solution.py:125
  128.4 6.5 %scatter_custom_fusion.2 = f32[676,128]{1,0:T(8,128)S(1)} fusion(f32[676,128]{1,0:T(8,128)S(1)} %scatter_custom_fusion.1, s32[1024]{0:T(1024)} %get-tuple-element.87, f32[1024,384]{1,0:T(8,128)S(1)} %fusion.39), kind=kCustom, calls=%fused_computation.18 | custom fusion | flops 131072 | bytes 870400 | tf_op jit(solution)/shard_map/scatter-add | solution.py:127
  135.2 1.3 collective-permute-start.5
  136.6 3.0 %collective-permute-start.4 = (bf16[1,2,24,128]{3,2,1,0:T(8,128)(2,1)S(1)}, bf16[1,2,24,128]{3,2,1,0:T(8,128)(2,1)S(1)}, u32[]{:S(2)}, u32[]{:S(2)}) collective-permute-start(bf16[1,2,24,128]{3,2,1,0:T(8,128)(2,1)S(1)} %maximum_bitcast_fusion), channel_id=1, source_target_pairs={{0,8},{8,16},{16,24},{1,9},{9,17},{17,25},{2,10},{10,18},{18,26},{... | collective-permute-start | bytes 36872 | tf_op jit(solution)/shard_map/ppermute | solution.py:12
  139.6 0.2 copy.52
  139.9 0.5 collective-permute-done.4
  140.4 1.3 collective-permute-start.6
  141.8 1.4 collective-permute-start.7
  143.3 0.8 copy.45
  144.3 0.8 copy.47
  145.0 0.6 convert_element_type.108
  145.6 2.1 collective-permute-done.7
  148.1 0.7 copy.44
  148.8 12.6 %reduce-scatter.14.cloned.1.call-done = bf16[32,128]{1,0:T(8,128)(2,1)} async-done(((bf16[128,128]{1,0:T(8,128)(2,1)}), bf16[32,128]{1,0:T(8,128)(2,1)}) %reduce-scatter.14.cloned.1.call-update) | async-done | bytes 8208 | tf_op jit(solution)/shard_map/reduce_scatter | solution.py:167
  161.4 1.3 convert_element_type.106
  162.7 21.1 %reduce-scatter.10.cloned.1.call-done = bf16[32,128]{1,0:T(8,128)(2,1)} async-done(((bf16[128,128]{1,0:T(8,128)(2,1)}), bf16[32,128]{1,0:T(8,128)(2,1)}) %reduce-scatter.10.cloned.1.call-update) | async-done | bytes 8208 | tf_op jit(solution)/shard_map/reduce_scatter | solution.py:161
  183.7 1.3 convert_element_type.102
  185.0 20.5 %reduce-scatter.12.cloned.1.call-done = bf16[64,128]{1,0:T(8,128)(2,1)} async-done(((bf16[256,128]{1,0:T(8,128)(2,1)}), bf16[64,128]{1,0:T(8,128)(2,1)}) %reduce-scatter.12.cloned.1.call-update) | async-done | bytes 16400 | tf_op jit(solution)/shard_map/reduce_scatter | solution.py:164
  205.6 1.3 convert_element_type.104
  206.9 20.5 %reduce-scatter.8.cloned.1.call-done = bf16[96,128]{1,0:T(8,128)(2,1)} async-done(((bf16[384,128]{1,0:T(8,128)(2,1)}), bf16[96,128]{1,0:T(8,128)(2,1)}) %reduce-scatter.8.cloned.1.call-update) | async-done | bytes 24592 | tf_op jit(solution)/shard_map/reduce_scatter | solution.py:158
  227.4 1.4 convert_element_type.100
  (86 shorter events, 1.6 us)
Async XLA Ops:
  7.2 33.3 %copy-start.2 = (bf16[24,24,128]{2,1,0:T(8,128)(2,1)S(1)}, bf16[24,24,128]{2,1,0:T(8,128)(2,1)}, u32[]{:S(2)}) copy-start(bf16[24,24,128]{2,1,0:T(8,128)(2,1)} %param.20) | copy-start | bytes 442372
  7.2 33.1 %copy-start.5 = (bf16[1024,128]{1,0:T(8,128)(2,1)S(1)}, bf16[1024,128]{1,0:T(8,128)(2,1)}, u32[]{:S(2)}) copy-start(bf16[1024,128]{1,0:T(8,128)(2,1)} %param.31) | copy-start | bytes 786436
  7.2 38.4 %copy-start.10 = (bf16[32,128]{1,0:T(8,128)(2,1)S(1)}, bf16[32,128]{1,0:T(8,128)(2,1)}, u32[]{:S(2)}) copy-start(bf16[32,128]{1,0:T(8,128)(2,1)} %param.28) | copy-start | bytes 24580
  7.2 137.0 %reduce-scatter.16.cloned.1.call-start = ((), (), s32[]{:S(2)}) async-start(), calls=%async_computation.9 | async-start | bytes 40960
  8.0 32.5 %collective-permute-start.1 = (bf16[1,24,128]{2,1,0:T(8,128)(2,1)S(1)}, bf16[1,24,128]{2,1,0:T(8,128)(2,1)S(1)}, u32[]{:S(2)}, u32[]{:S(2)}) collective-permute-start(bf16[1,24,128]{2,1,0:T(8,128)(2,1)S(1)} %get-tuple-element.98), channel_id=1, source_target_pairs={{8,0},{16,8},{24,16},{9,1},{17,9},{25,17},{10,2},{18,10},{26,18},{... | collective-permute-start | bytes 18440 | tf_op jit(solution)/shard_map/ppermute | solution.py:15
  9.3 31.2 %collective-permute-start = (bf16[1,24,128]{2,1,0:T(8,128)(2,1)S(1)}, bf16[1,24,128]{2,1,0:T(8,128)(2,1)S(1)}, u32[]{:S(2)}, u32[]{:S(2)}) collective-permute-start(bf16[1,24,128]{2,1,0:T(8,128)(2,1)S(1)} %get-tuple-element.99), channel_id=1, source_target_pairs={{0,8},{8,16},{16,24},{1,9},{9,17},{17,25},{2,10},{10,18},{18,26},{... | collective-permute-start | bytes 18440 | tf_op jit(solution)/shard_map/ppermute | solution.py:12
  18.8 39.5 %copy-start.8 = (f32[128]{0:T(128)}, f32[128]{0:T(128)S(1)}, u32[]{:S(2)}) copy-start(f32[128]{0:T(128)S(1)} %get-tuple-element.109) | copy-start | bytes 1540
  40.2 17.7 %copy-start.3 = (bf16[128,128]{1,0:T(8,128)(2,1)}, bf16[128,128]{1,0:T(8,128)(2,1)S(1)}, u32[]{:S(2)}) copy-start(bf16[128,128]{1,0:T(8,128)(2,1)S(1)} %all_gather.16) | copy-start | bytes 98308
  40.6 10.2 %collective-permute-start.2 = (bf16[26,1,128]{2,1,0:T(2,128)(2,1)S(1)}, bf16[26,1,128]{2,1,0:T(2,128)(2,1)S(1)}, u32[]{:S(2)}, u32[]{:S(2)}) collective-permute-start(bf16[26,1,128]{2,1,0:T(2,128)(2,1)S(1)} %get-tuple-element.96), channel_id=1, source_target_pairs={{0,1},{1,2},{2,3},{3,4},{4,5},{5,6},{6,7},{8,9},{9,10},{10,11},{11... | collective-permute-start | bytes 19976 | tf_op jit(solution)/shard_map/ppermute | solution.py:12
  44.2 6.5 %collective-permute-start.3 = (bf16[26,1,128]{2,1,0:T(2,128)(2,1)S(1)}, bf16[26,1,128]{2,1,0:T(2,128)(2,1)S(1)}, u32[]{:S(2)}, u32[]{:S(2)}) collective-permute-start(bf16[26,1,128]{2,1,0:T(2,128)(2,1)S(1)} %get-tuple-element.97), channel_id=1, source_target_pairs={{1,0},{2,1},{3,2},{4,3},{5,4},{6,5},{7,6},{9,8},{10,9},{11,10},{12... | collective-permute-start | bytes 19976 | tf_op jit(solution)/shard_map/ppermute | solution.py:15
  58.4 8.4 %copy-start = (bf16[24,24,128]{2,1,0:T(8,128)(2,1)S(1)}, bf16[24,24,128]{2,1,0:T(8,128)(2,1)}, u32[]{:S(2)}) copy-start(bf16[24,24,128]{2,1,0:T(8,128)(2,1)} %param.30) | copy-start | bytes 442372
  73.7 1.1 copy-start.9
  73.9 1.4 copy-start.4
  75.6 0.8 copy-start.11
  75.6 0.8 copy-start.6
  75.6 0.9 copy-start.7
  122.1 39.2 %reduce-scatter.14.cloned.1.call-start = ((), (), s32[]{:S(2)}) async-start(), calls=%async_computation.8 | async-start | bytes 40960 | tf_op jit(solution)/shard_map/reduce_scatter | solution.py:167
  135.1 48.6 %reduce-scatter.10.cloned.1.call-start = ((), (), s32[]{:S(2)}) async-start(), calls=%async_computation.6 | async-start | bytes 40960 | tf_op jit(solution)/shard_map/reduce_scatter | solution.py:161
  135.2 4.8 %collective-permute-start.5 = (bf16[1,2,24,128]{3,2,1,0:T(8,128)(2,1)S(1)}, bf16[1,2,24,128]{3,2,1,0:T(8,128)(2,1)S(1)}, u32[]{:S(2)}, u32[]{:S(2)}) collective-permute-start(bf16[1,2,24,128]{3,2,1,0:T(8,128)(2,1)S(1)} %maximum_bitcast_fusion.1), channel_id=1, source_target_pairs={{8,0},{16,8},{24,16},{9,1},{17,9},{25,17},{10,2},{18,10},{26,18},{... | collective-permute-start | bytes 36872 | tf_op jit(solution)/shard_map/ppermute | solution.py:15
  136.5 69.1 %reduce-scatter.12.cloned.1.call-start = ((), (), s32[]{:S(2)}) async-start(), calls=%async_computation.7 | async-start | bytes 81920 | tf_op jit(solution)/shard_map/reduce_scatter | solution.py:164
  136.6 3.9 %collective-permute-start.4 = (bf16[1,2,24,128]{3,2,1,0:T(8,128)(2,1)S(1)}, bf16[1,2,24,128]{3,2,1,0:T(8,128)(2,1)S(1)}, u32[]{:S(2)}, u32[]{:S(2)}) collective-permute-start(bf16[1,2,24,128]{3,2,1,0:T(8,128)(2,1)S(1)} %maximum_bitcast_fusion), channel_id=1, source_target_pairs={{0,8},{8,16},{16,24},{1,9},{9,17},{17,25},{2,10},{10,18},{18,26},{... | collective-permute-start | bytes 36872 | tf_op jit(solution)/shard_map/ppermute | solution.py:12
  139.9 87.5 %reduce-scatter.8.cloned.1.call-start = ((), (), s32[]{:S(2)}) async-start(), calls=%async_computation.5 | async-start | bytes 122880 | tf_op jit(solution)/shard_map/reduce_scatter | solution.py:158
  140.4 5.2 %collective-permute-start.6 = (bf16[4,1,24,128]{3,2,1,0:T(8,128)(2,1)S(1)}, bf16[4,1,24,128]{3,2,1,0:T(8,128)(2,1)S(1)}, u32[]{:S(2)}, u32[]{:S(2)}) collective-permute-start(bf16[4,1,24,128]{3,2,1,0:T(8,128)(2,1)S(1)} %get-tuple-element.102), channel_id=1, source_target_pairs={{0,1},{1,2},{2,3},{3,4},{4,5},{5,6},{6,7},{8,9},{9,10},{10,11},{11... | collective-permute-start | bytes 73736 | tf_op jit(solution)/shard_map/ppermute | solution.py:12
  141.7 6.3 %copy-start.1 = (f32[576,128]{1,0:T(8,128)S(1)}, f32[576,128]{1,0:T(8,128)}, u32[]{:S(2)}) copy-start(f32[576,128]{1,0:T(8,128)} %get-tuple-element.90) | copy-start | bytes 884740
  141.8 6.0 %collective-permute-start.7 = (bf16[4,1,24,128]{3,2,1,0:T(8,128)(2,1)S(1)}, bf16[4,1,24,128]{3,2,1,0:T(8,128)(2,1)S(1)}, u32[]{:S(2)}, u32[]{:S(2)}) collective-permute-start(bf16[4,1,24,128]{3,2,1,0:T(8,128)(2,1)S(1)} %get-tuple-element.103), channel_id=1, source_target_pairs={{1,0},{2,1},{3,2},{4,3},{5,4},{6,5},{7,6},{9,8},{10,9},{11,10},{12... | collective-permute-start | bytes 73736 | tf_op jit(solution)/shard_map/ppermute | solution.py:15
Sparse Core Ops, SparseCore 0:
  122.2 16.6 reduce-scatter.15
  142.0 19.3 reduce-scatter.13
  164.4 19.3 reduce-scatter.9
  186.1 19.3 reduce-scatter.11
  207.9 19.5 reduce-scatter.7
where the time goes:
time: 236 us; the launch traced here: 235 us
  waiting for transfers between devices  77.4 us (33%)
  blocking collectives  72.8 us (31%)
  other arithmetic  32.3 us (14%)
  local copies, waits for them, and re-layouts  16.5 us (7%)
  starting transfers between devices  16.5 us (7%)
  between operations  15.1 us (6%)
  matrix products  4.72 us (2%)
    psum x1, blocking collectives, shards(): lax.psum((local_terms[0], local_terms[1], local_terms[2], local_terms[3],...  44.8 us
    reduce_scatter x1, waiting for transfers between devices, shards(): lax.psum_scatter(summed[1].astype(jnp.bfloat16), 'dom', scatter_dimension...  21.1 us
    reduce_scatter x1, waiting for transfers between devices, shards(): lax.psum_scatter(summed[2].astype(jnp.bfloat16), 'dom', scatter_dimension...  20.5 us
    reduce_scatter x1, waiting for transfers between devices, shards(): lax.psum_scatter(summed[0].astype(jnp.bfloat16), 'dom', scatter_dimension...  20.5 us
    scatter-add x2, other arithmetic, shards(): spread = spread.at[source_pad].add(edge_in_grad[:, latent:2 * latent]).at...  12.8 us
    reduce_scatter x1, waiting for transfers between devices, shards(): lax.psum_scatter(summed[3].astype(jnp.bfloat16), 'dom', scatter_dimension...  12.6 us
    ppermute x4, starting transfers between devices, with_halo(): lax.ppermute(lax.slice_in_dim(block, block.shape[dim] - width, None, axis...  11 us
    scatter-add x1, other arithmetic, shards(): jax.ops.segment_sum(message * active, edge_dst, num_segments=block_side *...  6.48 us
  transfers between devices with their start and end apart: 13, of which 6 were waited for; matrix products, arithmetic and copies ran while one was open for 11% of the time, Pallas kernels for 0%

commit v1 on v0

v1 whole, which is shorter than its diff:
```python
import functools

import jax
import jax.numpy as jnp
from jax import lax
from jax.experimental import pallas as pl
from jax.experimental.pallas import tpu as pltpu
from jax.sharding import PartitionSpec as P

MESH = pl.DeviceIdType.MESH
BF = jnp.bfloat16
F32 = jnp.float32
LANES = 128


def ceil_to(value, step):
    return -(-value // step) * step


def mm(a, b):
    return jnp.dot(a, b, preferred_element_type=F32)


def mm_nt(a, b):
    return lax.dot_general(a, b, (((1,), (1,)), ((), ())), preferred_element_type=F32)


def mm_tn(a, b):
    return lax.dot_general(a, b, (((0,), (0,)), ((), ())), preferred_element_type=F32)


def iota(shape, dim):
    return lax.broadcasted_iota(jnp.int32, shape, dim)


def one_hot(mask):
    return jnp.where(mask, 1.0, 0.0).astype(BF)


def layer_norm(raw_out):
    average = jnp.mean(raw_out, axis=-1, keepdims=True)
    centered = raw_out - average
    inv_std = lax.rsqrt(jnp.mean(centered * centered, axis=-1, keepdims=True) + 1e-05)
    return centered * inv_std, inv_std


def norm_back(upstream, normed, inv_std):
    return (
        upstream
        - jnp.mean(upstream, axis=-1, keepdims=True)
        - normed * jnp.mean(upstream * normed, axis=-1, keepdims=True)
    ) * inv_std


def split_rows(total, step):
    return [(at, min(step, total - at)) for at in range(0, total, step)]


class Plan:
    def __init__(self, n_dom, n_sub, side, edges, latent, rows):
        self.n_dom, self.n_sub = n_dom, n_sub
        self.side, self.edges, self.latent = side, edges, latent
        self.nodes = side * side
        self.own = ceil_to(self.nodes, LANES)
        self.strip = ceil_to(side, 16)
        self.halo = ceil_to(4 * self.strip, LANES)
        self.rows = rows
        at = 0
        self.off = {}
        for name in ("node_in", "node_out", "edge_in", "edge_out", "gains"):
            self.off[name] = at
            at += 16 if name == "gains" else ceil_to(rows[name], 16)
        self.shard = at
        self.node_part = self.off["edge_in"]
        self.piece = ceil_to(-(-at // n_sub), 16)
        self.total = self.piece * n_sub


def kernel(
    plan,
    node_ref,
    feat_ref,
    dst_ref,
    dir_ref,
    count_ref,
    wei_ref,
    weo_ref,
    wni_ref,
    wno_ref,
    gains_ref,
    ncot_ref,
    ecot_ref,
    node_out,
    edge_out,
    gei_out,
    geo_out,
    gni_out,
    gno_out,
    gain_out,
    wbuf,
    own,
    halo,
    strips,
    gstrips,
    ghalo,
    s_dst,
    s_src,
    t_dst,
    t_src,
    x_e,
    hid_e,
    normed_e,
    inv_e,
    gpre_e,
    graw_e,
    agg,
    x_n,
    g1,
    r1,
    p2,
    r2,
    fin,
    w_send,
    w_recv,
    h_send,
    h_recv,
    b_send,
    b_recv,
    n_send,
    n_recv,
    e_send,
    e_recv,
    q_send,
    q_recv,
    f_send,
    f_recv,
):
    n_dom, n_sub, side, edges = plan.n_dom, plan.n_sub, plan.side, plan.edges
    nodes, n_own, strip, lat = plan.nodes, plan.own, plan.strip, plan.latent
    n_halo, off, rows = plan.halo, plan.off, plan.rows
    d = lax.axis_index("dom")
    s = lax.axis_index("sub")

    halo[...] = jnp.zeros_like(halo)
    ghalo[...] = jnp.zeros_like(ghalo)
    barrier = pltpu.get_barrier_semaphore()
    for k in range(1, n_dom):
        pl.semaphore_signal(
            barrier, inc=1, device_id={"dom": lax.rem(d + k, n_dom)}, device_id_type=MESH
        )
    for k in range(1, n_sub):
        pl.semaphore_signal(
            barrier, inc=1, device_id={"sub": lax.rem(s + k, n_sub)}, device_id_type=MESH
        )

    shard_refs = {"edge_in": wei_ref, "edge_out": weo_ref, "node_in": wni_ref, "node_out": wno_ref}
    for name, ref in shard_refs.items():
        wbuf[d, off[name] : off[name] + rows[name], :] = ref[...]
    width = gains_ref.shape[1]
    gains32 = gains_ref[...].astype(F32)
    row16 = iota((16, width), 0)
    gains16 = jnp.where(
        row16 == 0, gains32[0:1, :], jnp.where(row16 == 1, gains32[1:2, :], 0.0)
    ).astype(BF)
    place = one_hot(iota((width, lat), 1) == iota((width, lat), 0) + d * width)
    wbuf[d, off["gains"] : off["gains"] + 16, :] = mm(gains16, place).astype(BF)

    own[0:nodes, :] = node_ref[...]
    own[nodes:n_own, :] = jnp.zeros((n_own - nodes, lat), BF)
    pos = iota((strip, n_own), 0)
    node_id = iota((strip, n_own), 1)
    inside = pos < side
    borders = (pos, (side - 1) * side + pos, pos * side, pos * side + side - 1)
    for b in range(4):
        select = one_hot((node_id == borders[b]) & inside)
        strips[b * strip : (b + 1) * strip, :] = mm(select, own[...]).astype(BF)

    pl.semaphore_wait(barrier, (n_dom - 1) + (n_sub - 1))

    w_copies = []
    for k in range(1, n_dom):
        copy = pltpu.make_async_remote_copy(
            src_ref=wbuf.at[d],
            dst_ref=wbuf.at[d],
            send_sem=w_send.at[k],
            recv_sem=w_recv.at[k],
            device_id={"dom": lax.rem(d + k, n_dom)},
            device_id_type=MESH,
        )
        copy.start()
        w_copies.append(copy)

    low_d, high_d = d > 0, d < n_dom - 1
    low_s, high_s = s > 0, s < n_sub - 1
    down_d, up_d = {"dom": jnp.maximum(d - 1, 0)}, {"dom": jnp.minimum(d + 1, n_dom - 1)}
    down_s, up_s = {"sub": jnp.maximum(s - 1, 0)}, {"sub": jnp.minimum(s + 1, n_sub - 1)}

    def strip_copies(source, target, send, recv, devices):
        return [
            pltpu.make_async_remote_copy(
                src_ref=source.at[pl.ds(b * strip, strip)],
                dst_ref=target.at[pl.ds(b * strip, strip)],
                send_sem=send.at[b],
                recv_sem=recv.at[b],
                device_id=devices[b],
                device_id_type=MESH,
            )
            for b in range(4)
        ]

    def when_all(conditions, actions):
        for condition, action in zip(conditions, actions):
            pl.when(condition)(action)

    h_copies = strip_copies(strips, halo, h_send, h_recv, (down_d, up_d, down_s, up_s))
    h_to, h_from = (low_d, high_d, low_s, high_s), (high_d, low_d, high_s, low_s)
    when_all(h_to, [c.start for c in h_copies])

    count = count_ref[0]
    for j in range(edges // LANES):
        at = j * LANES
        dst = dst_ref[j : j + 1, :]
        direction = dir_ref[j : j + 1, :]
        row = jnp.floor((dst.astype(F32) + 0.5) * (1.0 / side)).astype(jnp.int32)
        col = dst - row * side
        src = jnp.where(
            direction == 0,
            jnp.where(row == side - 1, n_own + col, dst + side),
            jnp.where(
                direction == 1,
                jnp.where(row == 0, n_own + strip + col, dst - side),
                jnp.where(
                    direction == 2,
                    jnp.where(col == side - 1, n_own + 2 * strip + row, dst + 1),
                    jnp.where(col == 0, n_own + 3 * strip + row, dst - 1),
                ),
            ),
        )
        dst = jnp.where(iota((1, LANES), 1) + at < count, dst, -1)
        dst_cols = jnp.broadcast_to(dst, (LANES, LANES)).T
        src_cols = jnp.broadcast_to(src, (LANES, LANES)).T
        lane = iota((LANES, LANES), 1)
        for t in range((n_own + n_halo) // LANES):
            cut = slice(t * LANES, (t + 1) * LANES)
            s_src[at : at + LANES, cut] = one_hot(src_cols == lane + t * LANES)
            if t < n_own // LANES:
                s_dst[at : at + LANES, cut] = one_hot(dst_cols == lane + t * LANES)
        t_src[:, at : at + LANES] = one_hot(iota((n_own + n_halo, LANES), 0) == src)
        t_dst[:, at : at + LANES] = one_hot(iota((n_own, LANES), 0) == dst)

    x_e[:, 0:lat] = feat_ref[...]
    chunks = split_rows(edges, 256)
    for at, size in chunks:
        x_e[at : at + size, 2 * lat :] = mm(s_dst[at : at + size, :], own[...]).astype(BF)
        x_e[at : at + size, lat : 2 * lat] = mm(
            s_src[at : at + size, 0:n_own], own[...]
        ).astype(BF)

    when_all(h_from, [c.wait_recv for c in h_copies])
    for at, size in chunks:
        far = mm(s_src[at : at + size, n_own:], halo[...])
        x_e[at : at + size, lat : 2 * lat] = (
            x_e[at : at + size, lat : 2 * lat].astype(F32) + far
        ).astype(BF)
    for copy in w_copies:
        copy.wait_recv()

    def whole(name):
        at, size = off[name], rows[name]
        if size % 16 == 0:
            return jnp.concatenate([wbuf[n, at : at + size, :] for n in range(n_dom)], axis=0)
        padded = ceil_to(size, 16)
        parts = [wbuf[n, at : at + padded, :].astype(F32)[0:size, :] for n in range(n_dom)]
        return jnp.concatenate(parts, axis=0).astype(BF)

    w1e, w2e, w1n, w2n = whole("edge_in"), whole("edge_out"), whole("node_in"), whole("node_out")
    gains = sum(wbuf[n, off["gains"] : off["gains"] + 16, :].astype(F32) for n in range(n_dom))
    gain_edge, gain_node = gains[0:1, :], gains[1:2, :]

    total = jnp.zeros((n_own, lat), F32)
    for at, size in chunks:
        hidden = jnp.maximum(mm(x_e[at : at + size, :], w1e), 0.0).astype(BF)
        hid_e[at : at + size, :] = hidden
        normed, inv_std = layer_norm(mm(hidden, w2e))
        normed_e[at : at + size, :] = normed
        inv_e[at : at + size, :] = inv_std
        message = normed * gain_edge
        high = message.astype(BF)
        low = (message - high.astype(F32)).astype(BF)
        both = mm(t_dst[:, at : at + size], jnp.concatenate([high, low], axis=1))
        total = total + both[:, 0:lat] + both[:, lat:]
    agg[...] = total.astype(BF)

    scale = (n_dom * n_sub * nodes) ** -0.5
    node_first = jnp.zeros((2 * lat, lat), F32)
    node_second = jnp.zeros((lat, lat), F32)
    node_gain = jnp.zeros((1, lat), F32)
    x_n[:, 0:lat] = own[...]
    x_n[:, lat:] = agg[...]
    node_grads = []
    for at, size in split_rows(nodes, 192):
        inputs = x_n[at : at + size, :]
        hidden = jnp.maximum(mm(inputs, w1n), 0.0).astype(BF)
        normed, inv_std = layer_norm(mm(hidden, w2n))
        upstream = ncot_ref[at : at + size, :].astype(F32)
        node_gain += jnp.sum(upstream * normed, axis=0, keepdims=True)
        graw = norm_back(upstream * gain_node, normed, inv_std).astype(BF)
        node_second += mm_tn(hidden, graw)
        gpre = jnp.where(hidden > 0, mm_nt(graw, w2n), 0.0).astype(BF)
        node_first += mm_tn(inputs, gpre)
        grad_in = mm_nt(gpre, w1n)
        node_grads.append(upstream + grad_in[:, 0:lat])
        agg[at : at + size, :] = grad_in[:, lat:].astype(BF)

    def pack(name, value):
        size = rows[name]
        for n in range(n_dom):
            g1[n, off[name] : off[name] + size, :] = (
                value[n * size : (n + 1) * size, :] * scale
            ).astype(BF)
            if size % 16:
                end = off[name] + ceil_to(size, 16)
                g1[n, off[name] + size : end, :] = jnp.zeros((end - off[name] - size, lat), BF)

    def dom_copies(first, last, send, recv):
        copies = []
        for k in range(1, n_dom):
            peer = lax.rem(d + k, n_dom)
            copy = pltpu.make_async_remote_copy(
                src_ref=g1.at[peer, pl.ds(first, last - first)],
                dst_ref=r1.at[k, pl.ds(first, last - first)],
                send_sem=send.at[k],
                recv_sem=recv.at[k],
                device_id={"dom": peer},
                device_id_type=MESH,
            )
            copy.start()
            copies.append(copy)
        return copies

    pack("node_in", node_first)
    pack("node_out", node_second)
    n_copies = dom_copies(0, plan.node_part, n_send, n_recv)

    edge_gain = jnp.zeros((1, lat), F32)
    for at, size in chunks:
        cot = ecot_ref[at : at + size, :].astype(F32)
        live = iota((size, lat), 0) + at < count
        upstream = jnp.where(live, cot, 0.0) + mm(s_dst[at : at + size, :], agg[...])
        normed, inv_std = normed_e[at : at + size, :], inv_e[at : at + size, :]
        edge_gain += jnp.sum(upstream * normed, axis=0, keepdims=True)
        graw = norm_back(upstream * gain_edge, normed, inv_std).astype(BF)
        graw_e[at : at + size, :] = graw
        gpre = jnp.where(hid_e[at : at + size, :] > 0, mm_nt(graw, w2e), 0.0).astype(BF)
        gpre_e[at : at + size, :] = gpre
        edge_out[at : at + size, :] = (cot + mm_nt(gpre, w1e[0:lat, :])).astype(BF)

    w_src, w_dst = w1e[lat : 2 * lat, :], w1e[2 * lat :, :]
    back = mm(t_src[n_own:, :], gpre_e[...]).astype(BF)
    gstrips[...] = mm_nt(back, w_src).astype(BF)
    b_copies = strip_copies(gstrips, ghalo, b_send, b_recv, (up_d, down_d, up_s, down_s))
    when_all(h_from, [c.start for c in b_copies])

    pack("edge_in", mm_tn(x_e[...], gpre_e[...]))
    pack("edge_out", mm_tn(hid_e[...], graw_e[...]))
    row16 = iota((16, lat), 0)
    gains16 = jnp.where(row16 == 0, edge_gain, jnp.where(row16 == 1, node_gain, 0.0))
    for n in range(n_dom):
        g1[n, off["gains"] : off["gains"] + 16, :] = (gains16 * scale).astype(BF)
        if plan.total > plan.shard:
            g1[n, plan.shard :, :] = jnp.zeros((plan.total - plan.shard, lat), BF)
    e_copies = dom_copies(plan.node_part, plan.total, e_send, e_recv)

    at_src = mm(t_src[0:n_own, :], gpre_e[...]).astype(BF)
    at_dst = mm(t_dst[...], gpre_e[...]).astype(BF)
    spread = mm_nt(at_src, w_src) + mm_nt(at_dst, w_dst)

    for copy in n_copies + e_copies:
        copy.wait_recv()
    acc = g1[d].astype(F32)
    for k in range(1, n_dom):
        acc = acc + r1[k].astype(F32)
    p2[...] = acc.astype(BF).reshape(n_sub, plan.piece, lat)
    q_copies = []
    for k in range(1, n_sub):
        peer = lax.rem(s + k, n_sub)
        copy = pltpu.make_async_remote_copy(
            src_ref=p2.at[peer],
            dst_ref=r2.at[k],
            send_sem=q_send.at[k],
            recv_sem=q_recv.at[k],
            device_id={"sub": peer},
            device_id_type=MESH,
        )
        copy.start()
        q_copies.append(copy)

    when_all(h_to, [c.wait_recv for c in b_copies])
    pos = iota((n_own, n_halo), 1)
    node_id = iota((n_own, n_halo), 0)
    picked = jnp.zeros((n_own, n_halo), jnp.bool_)
    for b in range(4):
        at = pos - b * strip
        border = (at, (side - 1) * side + at, at * side, at * side + side - 1)[b]
        picked = picked | ((at >= 0) & (at < side) & (node_id == border))
    spread = spread + mm(one_hot(picked), ghalo[...])
    for i, (at, size) in enumerate(split_rows(nodes, 192)):
        node_out[at : at + size, :] = (node_grads[i] + spread[at : at + size, :]).astype(BF)

    for copy in q_copies:
        copy.wait_recv()
    acc = p2[s].astype(F32)
    for k in range(1, n_sub):
        acc = acc + r2[k].astype(F32)
    fin[s] = acc.astype(BF)
    f_copies = []
    for k in range(1, n_sub):
        copy = pltpu.make_async_remote_copy(
            src_ref=fin.at[s],
            dst_ref=fin.at[s],
            send_sem=f_send.at[k],
            recv_sem=f_recv.at[k],
            device_id={"sub": lax.rem(s + k, n_sub)},
            device_id_type=MESH,
        )
        copy.start()
        f_copies.append(copy)
    for copy in f_copies:
        copy.wait_recv()
    result = fin[...].reshape(plan.total, lat)
    for name, ref in (
        ("edge_in", gei_out),
        ("edge_out", geo_out),
        ("node_in", gni_out),
        ("node_out", gno_out),
    ):
        ref[...] = result[off[name] : off[name] + ceil_to(rows[name], 16), :].astype(F32)[
            0 : rows[name], :
        ]
    gain_out[...] = mm_nt(result[off["gains"] : off["gains"] + 16, :], place)[0:2, :]

    for copy in w_copies + n_copies + e_copies + q_copies + f_copies:
        copy.wait_send()
    when_all(h_to, [c.wait_send for c in h_copies])
    when_all(h_from, [c.wait_send for c in b_copies])


def shards(
    node_feat,
    edge_feat,
    edge_dst,
    edge_dir,
    edge_count,
    w_edge_in,
    w_edge_out,
    w_node_in,
    w_node_out,
    gains,
    node_cot,
    edge_cot,
):
    n_dom, n_sub = lax.axis_size("dom"), lax.axis_size("sub")
    side, _, lat = node_feat.shape
    edges = edge_feat.shape[0]
    rows = {
        "edge_in": w_edge_in.shape[0],
        "edge_out": w_edge_out.shape[0],
        "node_in": w_node_in.shape[0],
        "node_out": w_node_out.shape[0],
    }
    plan = Plan(n_dom, n_sub, side, edges, lat, rows)
    nodes, n_own, n_halo = plan.nodes, plan.own, plan.halo
    vmem = pl.BlockSpec(memory_space=pltpu.VMEM)
    smem = pl.BlockSpec(memory_space=pltpu.SMEM)
    table = n_own + n_halo
    dma = pltpu.SemaphoreType.DMA
    outs = pl.pallas_call(
        functools.partial(kernel, plan),
        out_shape=[
            jax.ShapeDtypeStruct((nodes, lat), BF),
            jax.ShapeDtypeStruct((edges, lat), BF),
            jax.ShapeDtypeStruct(w_edge_in.shape, F32),
            jax.ShapeDtypeStruct(w_edge_out.shape, F32),
            jax.ShapeDtypeStruct(w_node_in.shape, F32),
            jax.ShapeDtypeStruct(w_node_out.shape, F32),
            jax.ShapeDtypeStruct(gains.shape, F32),
        ],
        in_specs=[vmem] * 4 + [smem] + [vmem] * 7,
        out_specs=[vmem] * 7,
        scratch_shapes=[
            pltpu.VMEM((n_dom, plan.shard, lat), BF),
            pltpu.VMEM((n_own, lat), BF),
            pltpu.VMEM((n_halo, lat), BF),
            pltpu.VMEM((n_halo, lat), BF),
            pltpu.VMEM((n_halo, lat), BF),
            pltpu.VMEM((n_halo, lat), BF),
            pltpu.VMEM((edges, n_own), BF),
            pltpu.VMEM((edges, table), BF),
            pltpu.VMEM((n_own, edges), BF),
            pltpu.VMEM((table, edges), BF),
            pltpu.VMEM((edges, 3 * lat), BF),
            pltpu.VMEM((edges, lat), BF),
            pltpu.VMEM((edges, lat), F32),
            pltpu.VMEM((edges, 1), F32),
            pltpu.VMEM((edges, lat), BF),
            pltpu.VMEM((edges, lat), BF),
            pltpu.VMEM((n_own, lat), BF),
            pltpu.VMEM((n_own, 2 * lat), BF),
            pltpu.VMEM((n_dom, plan.total, lat), BF),
            pltpu.VMEM((n_dom, plan.total, lat), BF),
            pltpu.VMEM((n_sub, plan.piece, lat), BF),
            pltpu.VMEM((n_sub, plan.piece, lat), BF),
            pltpu.VMEM((n_sub, plan.piece, lat), BF),
            dma((n_dom,)),
            dma((n_dom,)),
            dma((4,)),
            dma((4,)),
            dma((4,)),
            dma((4,)),
            dma((n_dom,)),
            dma((n_dom,)),
            dma((n_dom,)),
            dma((n_dom,)),
            dma((n_sub,)),
            dma((n_sub,)),
            dma((n_sub,)),
            dma((n_sub,)),
        ],
        compiler_params=pltpu.CompilerParams(
            collective_id=0, has_side_effects=True, vmem_limit_bytes=48 * 1024 * 1024
        ),
        name="graph_layer_backward",
    )(
        node_feat.reshape(nodes, lat),
        edge_feat,
        edge_dst.reshape(edges // LANES, LANES),
        edge_dir.reshape(edges // LANES, LANES),
        edge_count,
        w_edge_in,
        w_edge_out,
        w_node_in,
        w_node_out,
        gains,
        node_cot.reshape(nodes, lat),
        edge_cot,
    )
    return (outs[0].reshape(node_feat.shape), *outs[1:])


def solution(mesh):
    in_specs = (
        P("dom", "sub", None),
        P(("dom", "sub"), None),
        P(("dom", "sub")),
        P(("dom", "sub")),
        P(("dom", "sub")),
        P("dom", None),
        P("dom", None),
        P("dom", None),
        P("dom", None),
        P(None, "dom"),
        P("dom", "sub", None),
        P(("dom", "sub"), None),
    )
    out_specs = (
        P("dom", "sub", None),
        P(("dom", "sub"), None),
        P("dom", None),
        P("dom", None),
        P("dom", None),
        P("dom", None),
        P(None, "dom"),
    )
    return jax.shard_map(shards, mesh=mesh, in_specs=in_specs, out_specs=out_specs, check_vma=False)
```

time: 236 us -> 43 us (0.18)
  waiting for transfers between devices: 77.4 us -> 0 us
  blocking collectives: 72.8 us -> 0 us
  other arithmetic: 32.3 us -> 0 us
  Pallas kernels: 0 us -> 28.9 us
  starting transfers between devices: 16.5 us -> 0 us
  between operations: 15.1 us -> 1.33 us
  matrix products: 4.72 us -> 0 us
  local copies, waits for them, and re-layouts: 16.5 us -> 12.3 us
    reduce_scatter x4 -> x0, waiting for transfers between devices: 74.7 us -> none  [the longest x1 21.1 us: shards(): lax.psum_scatter(summed[1].astype(jnp.bfloat16), 'dom', scatter_dimension...]
    psum x1 -> x0, blocking collectives: 44.8 us -> none  [shards(): lax.psum((local_terms[0], local_terms[1], local_terms[2], local_terms[3],...]
    pallas_call x0 -> x1, Pallas kernels: none -> 28.9 us  [shards(): pl.pallas_call(functools.partial(kernel, plan), out_shape=[jax.ShapeDtype...]
    all_gather x5 -> x0, blocking collectives: 28 us -> none  [the longest x1 6.38 us: shards(): lax.all_gather(gains, 'dom', axis=1, tiled=True)]
    scatter-add x5 -> x0, other arithmetic: 19.3 us -> none  [the longest x2 12.8 us: shards(): spread = spread.at[source_pad].add(edge_in_grad[:, latent:2 * latent]).at...]
    ppermute x8 -> x0, starting transfers between devices: 16.3 us -> none  [the longest x4 11 us: with_halo(): lax.ppermute(lax.slice_in_dim(block, block.shape[dim] - width, None, axis...]
    gather x4 -> x0, local copies, waits for them, and re-layouts: 9.42 us -> none  [the longest x1 3.21 us: shards(): padded[source_pad]]
    unnamed x38 -> x29, local copies, waits for them, and re-layouts: 4.78 us -> 12.3 us
  transfers between devices with their start and end apart: 13 -> 0, of which waited for: 6 -> 0; matrix products, arithmetic and copies ran while one was open for 11% -> 0% of each run, Pallas kernels for 0% -> 0%
where the time goes in v1:
time: 43 us; the launch traced here: 42.5 us
  Pallas kernels  28.9 us (67%)
  local copies, waits for them, and re-layouts  12.3 us (29%)
  between operations  1.33 us (3%)
    pallas_call x1, Pallas kernels, shards(): pl.pallas_call(functools.partial(kernel, plan), out_shape=[jax.ShapeDtype...  28.9 us
    unnamed x29, local copies, waits for them, and re-layouts  12.3 us

profile of v1, /device:TPU:0, one launch (start us, length us, event | category | flops | bytes accessed | tf_op | source)
XLA Modules:
  0.0 42.5 jit_solution(15194083479137840230)
XLA Ops:
  0.6 0.0 copy-start.6
  1.3 0.0 copy-start.10
  1.3 0.0 copy-done.6
  1.3 0.6 %copy-done.10 = bf16[2,32]{1,0:T(2,128)(2,1)S(1)} copy-done((bf16[2,32]{1,0:T(2,128)(2,1)S(1)}, bf16[2,32]{1,0:T(2,128)(2,1)}, u32[]{:S(2)}) %copy-start.10) | copy-done | bytes 152
  2.0 0.0 copy-start
  2.0 0.9 %copy-done = bf16[1024,128]{1,0:T(8,128)(2,1)S(1)} copy-done((bf16[1024,128]{1,0:T(8,128)(2,1)S(1)}, bf16[1024,128]{1,0:T(8,128)(2,1)}, u32[]{:S(2)}) %copy-start) | copy-done | bytes 262168
  2.9 0.0 copy-start.1
  2.9 0.9 %copy-done.1 = bf16[1024,128]{1,0:T(8,128)(2,1)S(1)} copy-done((bf16[1024,128]{1,0:T(8,128)(2,1)S(1)}, bf16[1024,128]{1,0:T(8,128)(2,1)}, u32[]{:S(2)}) %copy-start.1) | copy-done | bytes 262168
  3.9 0.0 copy-start.2
  3.9 0.9 %copy-done.2 = bf16[24,24,128]{2,1,0:T(8,128)(2,1)S(1)} copy-done((bf16[24,24,128]{2,1,0:T(8,128)(2,1)S(1)}, bf16[24,24,128]{2,1,0:T(8,128)(2,1)}, u32[]{:S(2)}) %copy-start.2) | copy-done | bytes 147480
  4.8 0.0 copy-start.3
  4.8 0.9 %copy-done.3 = bf16[24,24,128]{2,1,0:T(8,128)(2,1)S(1)} copy-done((bf16[24,24,128]{2,1,0:T(8,128)(2,1)S(1)}, bf16[24,24,128]{2,1,0:T(8,128)(2,1)}, u32[]{:S(2)}) %copy-start.3) | copy-done | bytes 147480
  5.7 0.0 copy-start.4
  5.7 0.7 %copy-done.4 = bf16[96,128]{1,0:T(8,128)(2,1)S(1)} copy-done((bf16[96,128]{1,0:T(8,128)(2,1)S(1)}, bf16[96,128]{1,0:T(8,128)(2,1)}, u32[]{:S(2)}) %copy-start.4) | copy-done | bytes 24600
  6.4 0.0 copy-start.5
  6.4 0.7 %copy-done.5 = bf16[64,128]{1,0:T(8,128)(2,1)S(1)} copy-done((bf16[64,128]{1,0:T(8,128)(2,1)S(1)}, bf16[64,128]{1,0:T(8,128)(2,1)}, u32[]{:S(2)}) %copy-start.5) | copy-done | bytes 16408
  7.1 0.0 copy-start.7
  7.1 0.7 %copy-done.7 = bf16[32,128]{1,0:T(8,128)(2,1)S(1)} copy-done((bf16[32,128]{1,0:T(8,128)(2,1)S(1)}, bf16[32,128]{1,0:T(8,128)(2,1)}, u32[]{:S(2)}) %copy-start.7) | copy-done | bytes 8216
  7.8 0.0 copy-start.8
  7.8 0.7 %copy-done.8 = s32[1024]{0:T(1024)S(1)} copy-done((s32[1024]{0:T(1024)S(1)}, s32[1024]{0:T(1024)}, u32[]{:S(2)}) %copy-start.8) | copy-done | bytes 4120
  8.5 0.0 copy-start.9
  8.5 0.7 %copy-done.9 = s32[1024]{0:T(1024)S(1)} copy-done((s32[1024]{0:T(1024)S(1)}, s32[1024]{0:T(1024)}, u32[]{:S(2)}) %copy-start.9) | copy-done | bytes 4120
  9.2 28.9 %graph_layer_backward.1 = (bf16[576,128]{1,0:T(8,128)(2,1)S(1)}, bf16[1024,128]{1,0:T(8,128)(2,1)S(1)}, f32[96,128]{1,0:T(8,128)S(1)}, f32[32,128]{1,0:T(8,128)S...) custom-call(bf16[576,128]{1,0:T(8,128)(2,1)S(1)} %bitcast.6, ...), custom_call_target="tpu_custom_call" | custom-call | tf_op jit(solution)/shard_map/graph_layer_backward/pallas_call | solution.py:477
  38.1 0.7 %copy.27 = bf16[24,24,128]{2,1,0:T(8,128)(2,1)} copy(bf16[24,24,128]{2,1,0:T(8,128)(2,1)S(1)} %bitcast.5) | data formatting | bytes 294912
  38.8 0.7 %copy.28 = bf16[1024,128]{1,0:T(8,128)(2,1)} copy(bf16[1024,128]{1,0:T(8,128)(2,1)S(1)} %get-tuple-element.29) | data formatting | bytes 524288
  39.5 0.6 %copy.29 = f32[96,128]{1,0:T(8,128)} copy(f32[96,128]{1,0:T(8,128)S(1)} %get-tuple-element.30) | data formatting | bytes 98304
  40.1 0.6 %copy.30 = f32[32,128]{1,0:T(8,128)} copy(f32[32,128]{1,0:T(8,128)S(1)} %get-tuple-element.31) | data formatting | bytes 32768
  40.7 0.6 %copy.31 = f32[64,128]{1,0:T(8,128)} copy(f32[64,128]{1,0:T(8,128)S(1)} %get-tuple-element.32) | data formatting | bytes 65536
  41.3 0.6 %copy.32 = f32[32,128]{1,0:T(8,128)} copy(f32[32,128]{1,0:T(8,128)S(1)} %get-tuple-element.33) | data formatting | bytes 32768
  41.9 0.6 %copy.33 = f32[2,32]{1,0:T(2,128)} copy(f32[2,32]{1,0:T(2,128)S(1)} %get-tuple-element.34) | data formatting | bytes 512
Async XLA Ops:
  0.6 0.7 %copy-start.6 = (bf16[32,128]{1,0:T(8,128)(2,1)S(1)}, bf16[32,128]{1,0:T(8,128)(2,1)}, u32[]{:S(2)}) copy-start(bf16[32,128]{1,0:T(8,128)(2,1)} %weo_ref.1) | copy-start | bytes 24580
  1.3 0.7 %copy-start.10 = (bf16[2,32]{1,0:T(2,128)(2,1)S(1)}, bf16[2,32]{1,0:T(2,128)(2,1)}, u32[]{:S(2)}) copy-start(bf16[2,32]{1,0:T(2,128)(2,1)} %gains_ref.1) | copy-start | bytes 388
  2.0 0.9 %copy-start = (bf16[1024,128]{1,0:T(8,128)(2,1)S(1)}, bf16[1024,128]{1,0:T(8,128)(2,1)}, u32[]{:S(2)}) copy-start(bf16[1024,128]{1,0:T(8,128)(2,1)} %feat_ref.1) | copy-start | bytes 786436
  2.9 0.9 %copy-start.1 = (bf16[1024,128]{1,0:T(8,128)(2,1)S(1)}, bf16[1024,128]{1,0:T(8,128)(2,1)}, u32[]{:S(2)}) copy-start(bf16[1024,128]{1,0:T(8,128)(2,1)} %ecot_ref.1) | copy-start | bytes 786436
  3.9 0.9 %copy-start.2 = (bf16[24,24,128]{2,1,0:T(8,128)(2,1)S(1)}, bf16[24,24,128]{2,1,0:T(8,128)(2,1)}, u32[]{:S(2)}) copy-start(bf16[24,24,128]{2,1,0:T(8,128)(2,1)} %param.12) | copy-start | bytes 442372
  4.8 0.9 %copy-start.3 = (bf16[24,24,128]{2,1,0:T(8,128)(2,1)S(1)}, bf16[24,24,128]{2,1,0:T(8,128)(2,1)}, u32[]{:S(2)}) copy-start(bf16[24,24,128]{2,1,0:T(8,128)(2,1)} %param.22) | copy-start | bytes 442372
  5.7 0.7 %copy-start.4 = (bf16[96,128]{1,0:T(8,128)(2,1)S(1)}, bf16[96,128]{1,0:T(8,128)(2,1)}, u32[]{:S(2)}) copy-start(bf16[96,128]{1,0:T(8,128)(2,1)} %wei_ref.1) | copy-start | bytes 73732
  6.4 0.7 %copy-start.5 = (bf16[64,128]{1,0:T(8,128)(2,1)S(1)}, bf16[64,128]{1,0:T(8,128)(2,1)}, u32[]{:S(2)}) copy-start(bf16[64,128]{1,0:T(8,128)(2,1)} %wni_ref.1) | copy-start | bytes 49156
  7.1 0.7 %copy-start.7 = (bf16[32,128]{1,0:T(8,128)(2,1)S(1)}, bf16[32,128]{1,0:T(8,128)(2,1)}, u32[]{:S(2)}) copy-start(bf16[32,128]{1,0:T(8,128)(2,1)} %wno_ref.1) | copy-start | bytes 24580
  7.8 0.7 %copy-start.8 = (s32[1024]{0:T(1024)S(1)}, s32[1024]{0:T(1024)}, u32[]{:S(2)}) copy-start(s32[1024]{0:T(1024)} %param.14) | copy-start | bytes 12292
  8.5 0.7 %copy-start.9 = (s32[1024]{0:T(1024)S(1)}, s32[1024]{0:T(1024)}, u32[]{:S(2)}) copy-start(s32[1024]{0:T(1024)} %param.15) | copy-start | bytes 12292

commit v2 on v1

--- a/solution.py
+++ b/solution.py
@@ -78,11 +78,37 @@
 
 def kernel(
     plan,
+    node_hbm,
+    feat_hbm,
+    dst_hbm,
+    dir_hbm,
+    count_ref,
+    wei_hbm,
+    weo_hbm,
+    wni_hbm,
+    wno_hbm,
+    gains_hbm,
+    ncot_hbm,
+    ecot_hbm,
+    node_out_hbm,
+    edge_out_hbm,
+    gei_out_hbm,
+    geo_out_hbm,
+    gni_out_hbm,
+    gno_out_hbm,
+    gain_out_hbm,
+    node_out,
+    edge_out,
+    gei_out,
+    geo_out,
+    gni_out,
+    gno_out,
+    gain_out,
+    out_sem,
     node_ref,
     feat_ref,
     dst_ref,
     dir_ref,
-    count_ref,
     wei_ref,
     weo_ref,
     wni_ref,
@@ -90,13 +116,7 @@
     gains_ref,
     ncot_ref,
     ecot_ref,
-    node_out,
-    edge_out,
-    gei_out,
-    geo_out,
-    gni_out,
-    gno_out,
-    gain_out,
+    in_sem,
     wbuf,
     own,
     halo,
@@ -113,6 +133,7 @@
     inv_e,
     gpre_e,
     graw_e,
+    msg,
     agg,
     x_n,
     g1,
@@ -141,6 +162,37 @@
     d = lax.axis_index("dom")
     s = lax.axis_index("sub")
 
+    pairs = (
+        (wei_hbm, wei_ref),
+        (weo_hbm, weo_ref),
+        (wni_hbm, wni_ref),
+        (wno_hbm, wno_ref),
+        (gains_hbm, gains_ref),
+        (node_hbm, node_ref),
+        (dst_hbm, dst_ref),
+        (dir_hbm, dir_ref),
+        (feat_hbm, feat_ref),
+        (ncot_hbm, ncot_ref),
+        (ecot_hbm, ecot_ref),
+    )
+    loads = [
+        pltpu.make_async_copy(hbm, ref, in_sem.at[i]) for i, (hbm, ref) in enumerate(pairs)
+    ]
+    for load in loads:
+        load.start()
+    pairs = (
+        (node_out, node_out_hbm),
+        (edge_out, edge_out_hbm),
+        (gei_out, gei_out_hbm),
+        (geo_out, geo_out_hbm),
+        (gni_out, gni_out_hbm),
+        (gno_out, gno_out_hbm),
+        (gain_out, gain_out_hbm),
+    )
+    stores = [
+        pltpu.make_async_copy(ref, hbm, out_sem.at[i]) for i, (ref, hbm) in enumerate(pairs)
+    ]
+
     halo[...] = jnp.zeros_like(halo)
     ghalo[...] = jnp.zeros_like(ghalo)
     barrier = pltpu.get_barrier_semaphore()
@@ -153,6 +205,8 @@
             barrier, inc=1, device_id={"sub": lax.rem(s + k, n_sub)}, device_id_type=MESH
         )
 
+    for load in loads[:5]:
+        load.wait()
     shard_refs = {"edge_in": wei_ref, "edge_out": weo_ref, "node_in": wni_ref, "node_out": wno_ref}
     for name, ref in shard_refs.items():
         wbuf[d, off[name] : off[name] + rows[name], :] = ref[...]
@@ -165,6 +219,7 @@
     place = one_hot(iota((width, lat), 1) == iota((width, lat), 0) + d * width)
     wbuf[d, off["gains"] : off["gains"] + 16, :] = mm(gains16, place).astype(BF)
 
+    loads[5].wait()
     own[0:nodes, :] = node_ref[...]
     own[nodes:n_own, :] = jnp.zeros((n_own - nodes, lat), BF)
     pos = iota((strip, n_own), 0)
@@ -216,6 +271,8 @@
     h_to, h_from = (low_d, high_d, low_s, high_s), (high_d, low_d, high_s, low_s)
     when_all(h_to, [c.start for c in h_copies])
 
+    for load in loads[6:9]:
+        load.wait()
     count = count_ref[0]
     for j in range(edges // LANES):
         at = j * LANES
@@ -277,7 +334,6 @@
     gains = sum(wbuf[n, off["gains"] : off["gains"] + 16, :].astype(F32) for n in range(n_dom))
     gain_edge, gain_node = gains[0:1, :], gains[1:2, :]
 
-    total = jnp.zeros((n_own, lat), F32)
     for at, size in chunks:
         hidden = jnp.maximum(mm(x_e[at : at + size, :], w1e), 0.0).astype(BF)
         hid_e[at : at + size, :] = hidden
@@ -286,11 +342,13 @@
         inv_e[at : at + size, :] = inv_std
         message = normed * gain_edge
         high = message.astype(BF)
-        low = (message - high.astype(F32)).astype(BF)
-        both = mm(t_dst[:, at : at + size], jnp.concatenate([high, low], axis=1))
-        total = total + both[:, 0:lat] + both[:, lat:]
-    agg[...] = total.astype(BF)
-
+        msg[at : at + size, 0:lat] = high
+        msg[at : at + size, lat:] = (message - high.astype(F32)).astype(BF)
+    both = mm(t_dst[...], msg[...])
+    agg[...] = (both[:, 0:lat] + both[:, lat:]).astype(BF)
+
+    for load in loads[9:]:
+        load.wait()
     scale = (n_dom * n_sub * nodes) ** -0.5
     node_first = jnp.zeros((2 * lat, lat), F32)
     node_second = jnp.zeros((lat, lat), F32)
@@ -353,13 +411,6 @@
         graw_e[at : at + size, :] = graw
         gpre = jnp.where(hid_e[at : at + size, :] > 0, mm_nt(graw, w2e), 0.0).astype(BF)
         gpre_e[at : at + size, :] = gpre
-        edge_out[at : at + size, :] = (cot + mm_nt(gpre, w1e[0:lat, :])).astype(BF)
-
-    w_src, w_dst = w1e[lat : 2 * lat, :], w1e[2 * lat :, :]
-    back = mm(t_src[n_own:, :], gpre_e[...]).astype(BF)
-    gstrips[...] = mm_nt(back, w_src).astype(BF)
-    b_copies = strip_copies(gstrips, ghalo, b_send, b_recv, (up_d, down_d, up_s, down_s))
-    when_all(h_from, [c.start for c in b_copies])
 
     pack("edge_in", mm_tn(x_e[...], gpre_e[...]))
     pack("edge_out", mm_tn(hid_e[...], graw_e[...]))
@@ -370,6 +421,18 @@
         if plan.total > plan.shard:
             g1[n, plan.shard :, :] = jnp.zeros((plan.total - plan.shard, lat), BF)
     e_copies = dom_copies(plan.node_part, plan.total, e_send, e_recv)
+
+    w_src, w_dst = w1e[lat : 2 * lat, :], w1e[2 * lat :, :]
+    back = mm(t_src[n_own:, :], gpre_e[...]).astype(BF)
+    gstrips[...] = mm_nt(back, w_src).astype(BF)
+    b_copies = strip_copies(gstrips, ghalo, b_send, b_recv, (up_d, down_d, up_s, down_s))
+    when_all(h_from, [c.start for c in b_copies])
+
+    for at, size in chunks:
+        cot = ecot_ref[at : at + size, :].astype(F32)
+        grad = mm_nt(gpre_e[at : at + size, :], w1e[0:lat, :])
+        edge_out[at : at + size, :] = (cot + grad).astype(BF)
+    stores[1].start()
 
     at_src = mm(t_src[0:n_own, :], gpre_e[...]).astype(BF)
     at_dst = mm(t_dst[...], gpre_e[...]).astype(BF)
@@ -406,6 +469,7 @@
     spread = spread + mm(one_hot(picked), ghalo[...])
     for i, (at, size) in enumerate(split_rows(nodes, 192)):
         node_out[at : at + size, :] = (node_grads[i] + spread[at : at + size, :]).astype(BF)
+    stores[0].start()
 
     for copy in q_copies:
         copy.wait_recv()
@@ -438,11 +502,26 @@
             0 : rows[name], :
         ]
     gain_out[...] = mm_nt(result[off["gains"] : off["gains"] + 16, :], place)[0:2, :]
+    for store in stores[2:]:
+        store.start()
 
     for copy in w_copies + n_copies + e_copies + q_copies + f_copies:
         copy.wait_send()
     when_all(h_to, [c.wait_send for c in h_copies])
     when_all(h_from, [c.wait_send for c in b_copies])
+    for store in stores:
+        store.wait()
+
+
+def write_out(*refs):
+    sources, targets, sem = refs[:7], refs[7:14], refs[14]
+    copies = [
+        pltpu.make_async_copy(a, b, sem.at[i]) for i, (a, b) in enumerate(zip(sources, targets))
+    ]
+    for copy in copies:
+        copy.start()
+    for copy in copies:
+        copy.wait()
 
 
 def shards(
@@ -470,24 +549,39 @@
     }
     plan = Plan(n_dom, n_sub, side, edges, lat, rows)
     nodes, n_own, n_halo = plan.nodes, plan.own, plan.halo
-    vmem = pl.BlockSpec(memory_space=pltpu.VMEM)
-    smem = pl.BlockSpec(memory_space=pltpu.SMEM)
     table = n_own + n_halo
     dma = pltpu.SemaphoreType.DMA
+    hbm = pl.BlockSpec(memory_space=pltpu.HBM)
+    vmem_limit = 64 * 1024 * 1024
+    out_shape = [
+        jax.ShapeDtypeStruct((nodes, lat), BF),
+        jax.ShapeDtypeStruct((edges, lat), BF),
+        jax.ShapeDtypeStruct(w_edge_in.shape, F32),
+        jax.ShapeDtypeStruct(w_edge_out.shape, F32),
+        jax.ShapeDtypeStruct(w_node_in.shape, F32),
+        jax.ShapeDtypeStruct(w_node_out.shape, F32),
+        jax.ShapeDtypeStruct(gains.shape, F32),
+    ]
     outs = pl.pallas_call(
         functools.partial(kernel, plan),
-        out_shape=[
-            jax.ShapeDtypeStruct((nodes, lat), BF),
-            jax.ShapeDtypeStruct((edges, lat), BF),
-            jax.ShapeDtypeStruct(w_edge_in.shape, F32),
-            jax.ShapeDtypeStruct(w_edge_out.shape, F32),
-            jax.ShapeDtypeStruct(w_node_in.shape, F32),
-            jax.ShapeDtypeStruct(w_node_out.shape, F32),
-            jax.ShapeDtypeStruct(gains.shape, F32),
-        ],
-        in_specs=[vmem] * 4 + [smem] + [vmem] * 7,
-        out_specs=[vmem] * 7,
-        scratch_shapes=[
+        out_shape=out_shape,
+        in_specs=[hbm] * 4 + [pl.BlockSpec(memory_space=pltpu.SMEM)] + [hbm] * 7,
+        out_specs=[hbm] * 7,
+        scratch_shapes=[pltpu.VMEM(out.shape, out.dtype) for out in out_shape]
+        + [
+            dma((7,)),
+            pltpu.VMEM((nodes, lat), BF),
+            pltpu.VMEM((edges, lat), BF),
+            pltpu.VMEM((edges // LANES, LANES), jnp.int32),
+            pltpu.VMEM((edges // LANES, LANES), jnp.int32),
+            pltpu.VMEM(w_edge_in.shape, BF),
+            pltpu.VMEM(w_edge_out.shape, BF),
+            pltpu.VMEM(w_node_in.shape, BF),
+            pltpu.VMEM(w_node_out.shape, BF),
+            pltpu.VMEM(gains.shape, BF),
+            pltpu.VMEM((nodes, lat), BF),
+            pltpu.VMEM((edges, lat), BF),
+            dma((11,)),
             pltpu.VMEM((n_dom, plan.shard, lat), BF),
             pltpu.VMEM((n_own, lat), BF),
             pltpu.VMEM((n_halo, lat), BF),
@@ -504,6 +598,7 @@
             pltpu.VMEM((edges, 1), F32),
             pltpu.VMEM((edges, lat), BF),
             pltpu.VMEM((edges, lat), BF),
+            pltpu.VMEM((edges, 2 * lat), BF),
             pltpu.VMEM((n_own, lat), BF),
             pltpu.VMEM((n_own, 2 * lat), BF),
             pltpu.VMEM((n_dom, plan.total, lat), BF),
@@ -527,7 +622,7 @@
             dma((n_sub,)),
         ],
         compiler_params=pltpu.CompilerParams(
-            collective_id=0, has_side_effects=True, vmem_limit_bytes=48 * 1024 * 1024
+            collective_id=0, has_side_effects=True, vmem_limit_bytes=vmem_limit
         ),
         name="graph_layer_backward",
     )(
@@ -544,6 +639,15 @@
         node_cot.reshape(nodes, lat),
         edge_cot,
     )
+    outs = pl.pallas_call(
+        write_out,
+        out_shape=out_shape,
+        in_specs=[hbm] * 7,
+        out_specs=[hbm] * 7,
+        scratch_shapes=[dma((7,))],
+        compiler_params=pltpu.CompilerParams(vmem_limit_bytes=vmem_limit),
+        name="write_results",
+    )(*outs)
     return (outs[0].reshape(node_feat.shape), *outs[1:])
 
 

time: 43 us -> 47.4 us (1.10)
  Pallas kernels: 28.9 us -> 45.9 us
  local copies, waits for them, and re-layouts: 12.3 us -> 0 us
    pallas_call x1 -> x2, Pallas kernels: 28.9 us -> 45.9 us  [the longest x1 28.9 us: shards(): pl.pallas_call(functools.partial(kernel, plan), out_shape=out_shape, in_s...]
    unnamed x29 -> x0, local copies, waits for them, and re-layouts: 12.3 us -> none
where the time goes in v2:
time: 47.4 us; the launch traced here: 47.2 us
  Pallas kernels  45.9 us (97%)
  between operations  1.29 us (3%)
    pallas_call x1, Pallas kernels, shards(): pl.pallas_call(functools.partial(kernel, plan), out_shape=out_shape, in_s...  28.9 us
    pallas_call x1, Pallas kernels, shards(): pl.pallas_call(write_out, out_shape=out_shape, in_specs=[hbm] * 7, out_sp...  17.1 us

profile of v2, /device:TPU:0, one launch (start us, length us, event | category | flops | bytes accessed | tf_op | source)
XLA Modules:
  0.0 47.2 jit_solution(263996788760017609)
XLA Ops:
  1.3 28.9 %graph_layer_backward.1 = (bf16[576,128]{1,0:T(8,128)(2,1)}, bf16[1024,128]{1,0:T(8,128)(2,1)}, f32[96,128]{1,0:T(8,128)}, f32[32,128]{1,0:T(8,128)}, f32[64,128...) custom-call(bf16[576,128]{1,0:T(8,128)(2,1)} %bitcast.5, bf16[1024,128]{1,0:T(8,128)(2,1)} %feat_hbm.1, ...), custom_call_target="tpu_custom_call" | custom-call | tf_op jit(solution)/shard_map/graph_layer_backward/pallas_call | solution.py:565
  30.2 17.1 %write_results.1 = (bf16[576,128]{1,0:T(8,128)(2,1)}, bf16[1024,128]{1,0:T(8,128)(2,1)}, f32[96,128]{1,0:T(8,128)}, f32[32,128]{1,0:T(8,128)}, f32[64,128]{1,0:T...) custom-call(bf16[576,128]{1,0:T(8,128)(2,1)} %get-tuple-element.21.refs_0_, bf16[1024,128]{1,0:T(8,128)(2,1)} %get-tuple-element.22.refs_1_, ...), custom_call_target="tpu_custom_call" | custom-call | tf_op jit(solution)/shard_map/write_results/pallas_call | solution.py:642

commit v3 on v2

--- a/solution.py
+++ b/solution.py
@@ -52,8 +52,12 @@
     ) * inv_std
 
 
-def split_rows(total, step):
-    return [(at, min(step, total - at)) for at in range(0, total, step)]
+def each_chunk(total, step, body, init=0):
+    def turn(i, carry):
+        at = pl.multiple_of(i * step, step)
+        return body(pl.ds(at, step), at, carry)
+
+    return lax.fori_loop(0, total // step, turn, init)
 
 
 class Plan:
@@ -136,6 +140,10 @@
     msg,
     agg,
     x_n,
+    hid_n,
+    graw_n,
+    gpre_n,
+    node_acc,
     g1,
     r1,
     p2,
@@ -274,10 +282,12 @@
     for load in loads[6:9]:
         load.wait()
     count = count_ref[0]
-    for j in range(edges // LANES):
-        at = j * LANES
-        dst = dst_ref[j : j + 1, :]
-        direction = dir_ref[j : j + 1, :]
+    step = 256 if edges % 256 == 0 else LANES
+
+    def indices(cut_e, at, carry):
+        line = pl.ds(at // LANES, 1)
+        dst = dst_ref[line, :]
+        direction = dir_ref[line, :]
         row = jnp.floor((dst.astype(F32) + 0.5) * (1.0 / side)).astype(jnp.int32)
         col = dst - row * side
         src = jnp.where(
@@ -299,26 +309,32 @@
         lane = iota((LANES, LANES), 1)
         for t in range((n_own + n_halo) // LANES):
             cut = slice(t * LANES, (t + 1) * LANES)
-            s_src[at : at + LANES, cut] = one_hot(src_cols == lane + t * LANES)
+            s_src[cut_e, cut] = one_hot(src_cols == lane + t * LANES)
             if t < n_own // LANES:
-                s_dst[at : at + LANES, cut] = one_hot(dst_cols == lane + t * LANES)
-        t_src[:, at : at + LANES] = one_hot(iota((n_own + n_halo, LANES), 0) == src)
-        t_dst[:, at : at + LANES] = one_hot(iota((n_own, LANES), 0) == dst)
-
+                s_dst[cut_e, cut] = one_hot(dst_cols == lane + t * LANES)
+        t_src[:, cut_e] = one_hot(iota((n_own + n_halo, LANES), 0) == src)
+        t_dst[:, cut_e] = one_hot(iota((n_own, LANES), 0) == dst)
+        return carry
+
+    each_chunk(edges, LANES, indices)
     x_e[:, 0:lat] = feat_ref[...]
-    chunks = split_rows(edges, 256)
-    for at, size in chunks:
-        x_e[at : at + size, 2 * lat :] = mm(s_dst[at : at + size, :], own[...]).astype(BF)
-        x_e[at : at + size, lat : 2 * lat] = mm(
-            s_src[at : at + size, 0:n_own], own[...]
-        ).astype(BF)
+
+    def gather(cut, at, carry):
+        x_e[cut, 2 * lat :] = mm(s_dst[cut, :], own[...]).astype(BF)
+        x_e[cut, lat : 2 * lat] = mm(s_src[cut, 0:n_own], own[...]).astype(BF)
+        return carry
+
+    each_chunk(edges, step, gather)
 
     when_all(h_from, [c.wait_recv for c in h_copies])
-    for at, size in chunks:
-        far = mm(s_src[at : at + size, n_own:], halo[...])
-        x_e[at : at + size, lat : 2 * lat] = (
-            x_e[at : at + size, lat : 2 * lat].astype(F32) + far
-        ).astype(BF)
+
+    def gather_far(cut, at, carry):
+        far = mm(s_src[cut, n_own:], halo[...])
+        near = x_e[cut, lat : 2 * lat].astype(F32)
+        x_e[cut, lat : 2 * lat] = (near + far).astype(BF)
+        return carry
+
+    each_chunk(edges, step, gather_far)
     for copy in w_copies:
         copy.wait_recv()
 
@@ -334,41 +350,45 @@
     gains = sum(wbuf[n, off["gains"] : off["gains"] + 16, :].astype(F32) for n in range(n_dom))
     gain_edge, gain_node = gains[0:1, :], gains[1:2, :]
 
-    for at, size in chunks:
-        hidden = jnp.maximum(mm(x_e[at : at + size, :], w1e), 0.0).astype(BF)
-        hid_e[at : at + size, :] = hidden
+    def edge_forward(cut, at, carry):
+        hidden = jnp.maximum(mm(x_e[cut, :], w1e), 0.0).astype(BF)
+        hid_e[cut, :] = hidden
         normed, inv_std = layer_norm(mm(hidden, w2e))
-        normed_e[at : at + size, :] = normed
-        inv_e[at : at + size, :] = inv_std
+        normed_e[cut, :] = normed
+        inv_e[cut, :] = inv_std
         message = normed * gain_edge
         high = message.astype(BF)
-        msg[at : at + size, 0:lat] = high
-        msg[at : at + size, lat:] = (message - high.astype(F32)).astype(BF)
+        msg[cut, 0:lat] = high
+        msg[cut, lat:] = (message - high.astype(F32)).astype(BF)
+        return carry
+
+    each_chunk(edges, step, edge_forward)
     both = mm(t_dst[...], msg[...])
     agg[...] = (both[:, 0:lat] + both[:, lat:]).astype(BF)
 
     for load in loads[9:]:
         load.wait()
     scale = (n_dom * n_sub * nodes) ** -0.5
-    node_first = jnp.zeros((2 * lat, lat), F32)
-    node_second = jnp.zeros((lat, lat), F32)
-    node_gain = jnp.zeros((1, lat), F32)
     x_n[:, 0:lat] = own[...]
     x_n[:, lat:] = agg[...]
-    node_grads = []
-    for at, size in split_rows(nodes, 192):
-        inputs = x_n[at : at + size, :]
+
+    def node_both(cut, at, gain_sum):
+        inputs = x_n[cut, :]
         hidden = jnp.maximum(mm(inputs, w1n), 0.0).astype(BF)
         normed, inv_std = layer_norm(mm(hidden, w2n))
-        upstream = ncot_ref[at : at + size, :].astype(F32)
-        node_gain += jnp.sum(upstream * normed, axis=0, keepdims=True)
+        upstream = ncot_ref[cut, :].astype(F32)
         graw = norm_back(upstream * gain_node, normed, inv_std).astype(BF)
-        node_second += mm_tn(hidden, graw)
         gpre = jnp.where(hidden > 0, mm_nt(graw, w2n), 0.0).astype(BF)
-        node_first += mm_tn(inputs, gpre)
+        hid_n[cut, :] = hidden
+        graw_n[cut, :] = graw
+        gpre_n[cut, :] = gpre
         grad_in = mm_nt(gpre, w1n)
-        node_grads.append(upstream + grad_in[:, 0:lat])
-        agg[at : at + size, :] = grad_in[:, lat:].astype(BF)
+        node_acc[cut, :] = upstream + grad_in[:, 0:lat]
+        agg[cut, :] = grad_in[:, lat:].astype(BF)
+        return gain_sum + jnp.sum(upstream * normed, axis=0, keepdims=True)
+
+    node_step = max(n for n in range(16, 193, 16) if nodes % n == 0)
+    node_gain = each_chunk(nodes, node_step, node_both, jnp.zeros((1, lat), F32))
 
     def pack(name, value):
         size = rows[name]
@@ -396,21 +416,21 @@
             copies.append(copy)
         return copies
 
-    pack("node_in", node_first)
-    pack("node_out", node_second)
+    pack("node_in", mm_tn(x_n[0:nodes, :], gpre_n[...]))
+    pack("node_out", mm_tn(hid_n[...], graw_n[...]))
     n_copies = dom_copies(0, plan.node_part, n_send, n_recv)
 
-    edge_gain = jnp.zeros((1, lat), F32)
-    for at, size in chunks:
-        cot = ecot_ref[at : at + size, :].astype(F32)
-        live = iota((size, lat), 0) + at < count
-        upstream = jnp.where(live, cot, 0.0) + mm(s_dst[at : at + size, :], agg[...])
-        normed, inv_std = normed_e[at : at + size, :], inv_e[at : at + size, :]
-        edge_gain += jnp.sum(upstream * normed, axis=0, keepdims=True)
+    def edge_backward(cut, at, gain_sum):
+        cot = ecot_ref[cut, :].astype(F32)
+        live = iota((step, lat), 0) + at < count
+        upstream = jnp.where(live, cot, 0.0) + mm(s_dst[cut, :], agg[...])
+        normed, inv_std = normed_e[cut, :], inv_e[cut, :]
         graw = norm_back(upstream * gain_edge, normed, inv_std).astype(BF)
-        graw_e[at : at + size, :] = graw
-        gpre = jnp.where(hid_e[at : at + size, :] > 0, mm_nt(graw, w2e), 0.0).astype(BF)
-        gpre_e[at : at + size, :] = gpre
+        graw_e[cut, :] = graw
+        gpre_e[cut, :] = jnp.where(hid_e[cut, :] > 0, mm_nt(graw, w2e), 0.0).astype(BF)
+        return gain_sum + jnp.sum(upstream * normed, axis=0, keepdims=True)
+
+    edge_gain = each_chunk(edges, step, edge_backward, jnp.zeros((1, lat), F32))
 
     pack("edge_in", mm_tn(x_e[...], gpre_e[...]))
     pack("edge_out", mm_tn(hid_e[...], graw_e[...]))
@@ -428,10 +448,13 @@
     b_copies = strip_copies(gstrips, ghalo, b_send, b_recv, (up_d, down_d, up_s, down_s))
     when_all(h_from, [c.start for c in b_copies])
 
-    for at, size in chunks:
-        cot = ecot_ref[at : at + size, :].astype(F32)
-        grad = mm_nt(gpre_e[at : at + size, :], w1e[0:lat, :])
-        edge_out[at : at + size, :] = (cot + grad).astype(BF)
+
+    def edge_result(cut, at, carry):
+        grad = mm_nt(gpre_e[cut, :], w1e[0:lat, :])
+        edge_out[cut, :] = (ecot_ref[cut, :].astype(F32) + grad).astype(BF)
+        return carry
+
+    each_chunk(edges, step, edge_result)
     stores[1].start()
 
     at_src = mm(t_src[0:n_own, :], gpre_e[...]).astype(BF)
@@ -467,8 +490,7 @@
         border = (at, (side - 1) * side + at, at * side, at * side + side - 1)[b]
         picked = picked | ((at >= 0) & (at < side) & (node_id == border))
     spread = spread + mm(one_hot(picked), ghalo[...])
-    for i, (at, size) in enumerate(split_rows(nodes, 192)):
-        node_out[at : at + size, :] = (node_grads[i] + spread[at : at + size, :]).astype(BF)
+    node_out[...] = (node_acc[...] + spread[0:nodes, :]).astype(BF)
     stores[0].start()
 
     for copy in q_copies:
@@ -514,14 +536,16 @@
 
 
 def write_out(*refs):
-    sources, targets, sem = refs[:7], refs[7:14], refs[14]
-    copies = [
-        pltpu.make_async_copy(a, b, sem.at[i]) for i, (a, b) in enumerate(zip(sources, targets))
-    ]
-    for copy in copies:
-        copy.start()
-    for copy in copies:
-        copy.wait()
+    sources, targets, stage, in_sem, out_sem = refs[:7], refs[7:14], refs[14:21], *refs[21:]
+    reads = [pltpu.make_async_copy(sources[i], stage[i], in_sem.at[i]) for i in range(7)]
+    writes = [pltpu.make_async_copy(stage[i], targets[i], out_sem.at[i]) for i in range(7)]
+    for read in reads:
+        read.start()
+    for read, write in zip(reads, writes):
+        read.wait()
+        write.start()
+    for write in writes:
+        write.wait()
 
 
 def shards(
@@ -601,6 +625,10 @@
             pltpu.VMEM((edges, 2 * lat), BF),
             pltpu.VMEM((n_own, lat), BF),
             pltpu.VMEM((n_own, 2 * lat), BF),
+            pltpu.VMEM((nodes, lat), BF),
+            pltpu.VMEM((nodes, lat), BF),
+            pltpu.VMEM((nodes, lat), BF),
+            pltpu.VMEM((nodes, lat), F32),
             pltpu.VMEM((n_dom, plan.total, lat), BF),
             pltpu.VMEM((n_dom, plan.total, lat), BF),
             pltpu.VMEM((n_sub, plan.piece, lat), BF),
@@ -644,7 +672,8 @@
         out_shape=out_shape,
         in_specs=[hbm] * 7,
         out_specs=[hbm] * 7,
-        scratch_shapes=[dma((7,))],
+        scratch_shapes=[pltpu.VMEM(out.shape, out.dtype) for out in out_shape]
+        + [dma((7,)), dma((7,))],
         compiler_params=pltpu.CompilerParams(vmem_limit_bytes=vmem_limit),
         name="write_results",
     )(*outs)

time: 47.4 us -> 35.2 us (0.74)
  Pallas kernels: 45.9 us -> 33.7 us
    pallas_call x1, Pallas kernels: 17.1 us -> 1.88 us  [shards(): pl.pallas_call(write_out, out_shape=out_shape, in_specs=[hbm] * 7, out_sp...]
    pallas_call x1, Pallas kernels: 28.9 us -> 31.9 us  [shards(): pl.pallas_call(functools.partial(kernel, plan), out_shape=out_shape, in_s...]
where the time goes in v3:
time: 35.2 us; the launch traced here: 35 us
  Pallas kernels  33.7 us (96%)
  between operations  1.29 us (4%)
    pallas_call x1, Pallas kernels, shards(): pl.pallas_call(functools.partial(kernel, plan), out_shape=out_shape, in_s...  31.9 us
    pallas_call x1, Pallas kernels, shards(): pl.pallas_call(write_out, out_shape=out_shape, in_specs=[hbm] * 7, out_sp...  1.88 us

profile of v3, /device:TPU:0, one launch (start us, length us, event | category | flops | bytes accessed | tf_op | source)
XLA Modules:
  0.0 35.0 jit_solution(4677534110087693672)
XLA Ops:
  1.3 31.9 %graph_layer_backward.1 = (bf16[576,128]{1,0:T(8,128)(2,1)}, bf16[1024,128]{1,0:T(8,128)(2,1)}, f32[96,128]{1,0:T(8,128)}, f32[32,128]{1,0:T(8,128)}, f32[64,128...) custom-call(bf16[576,128]{1,0:T(8,128)(2,1)} %bitcast.5, bf16[1024,128]{1,0:T(8,128)(2,1)} %feat_hbm.1, ...), custom_call_target="tpu_custom_call" | custom-call | tf_op jit(solution)/shard_map/graph_layer_backward/pallas_call | solution.py:589
  33.2 1.9 %write_results.1 = (bf16[576,128]{1,0:T(8,128)(2,1)}, bf16[1024,128]{1,0:T(8,128)(2,1)}, f32[96,128]{1,0:T(8,128)}, f32[32,128]{1,0:T(8,128)}, f32[64,128]{1,0:T...) custom-call(bf16[576,128]{1,0:T(8,128)(2,1)} %get-tuple-element.21.refs_0_, bf16[1024,128]{1,0:T(8,128)(2,1)} %get-tuple-element.22.refs_1_, ...), custom_call_target="tpu_custom_call" | custom-call | tf_op jit(solution)/shard_map/write_results/pallas_call | solution.py:670

commit v4 on v3

--- a/solution.py
+++ b/solution.py
@@ -53,11 +53,10 @@
 
 
 def each_chunk(total, step, body, init=0):
-    def turn(i, carry):
-        at = pl.multiple_of(i * step, step)
-        return body(pl.ds(at, step), at, carry)
-
-    return lax.fori_loop(0, total // step, turn, init)
+    carry = init
+    for at in range(0, total, step):
+        carry = body(slice(at, at + step), at, carry)
+    return carry
 
 
 class Plan:
@@ -122,8 +121,7 @@
     ecot_ref,
     in_sem,
     wbuf,
-    own,
-    halo,
+    table,
     strips,
     gstrips,
     ghalo,
@@ -201,7 +199,7 @@
         pltpu.make_async_copy(ref, hbm, out_sem.at[i]) for i, (ref, hbm) in enumerate(pairs)
     ]
 
-    halo[...] = jnp.zeros_like(halo)
+    table[n_own:, :] = jnp.zeros((n_halo, lat), BF)
     ghalo[...] = jnp.zeros_like(ghalo)
     barrier = pltpu.get_barrier_semaphore()
     for k in range(1, n_dom):
@@ -228,15 +226,15 @@
     wbuf[d, off["gains"] : off["gains"] + 16, :] = mm(gains16, place).astype(BF)
 
     loads[5].wait()
-    own[0:nodes, :] = node_ref[...]
-    own[nodes:n_own, :] = jnp.zeros((n_own - nodes, lat), BF)
+    table[0:nodes, :] = node_ref[...]
+    table[nodes:n_own, :] = jnp.zeros((n_own - nodes, lat), BF)
     pos = iota((strip, n_own), 0)
     node_id = iota((strip, n_own), 1)
     inside = pos < side
     borders = (pos, (side - 1) * side + pos, pos * side, pos * side + side - 1)
     for b in range(4):
         select = one_hot((node_id == borders[b]) & inside)
-        strips[b * strip : (b + 1) * strip, :] = mm(select, own[...]).astype(BF)
+        strips[b * strip : (b + 1) * strip, :] = mm(select, table[0:n_own, :]).astype(BF)
 
     pl.semaphore_wait(barrier, (n_dom - 1) + (n_sub - 1))
 
@@ -258,11 +256,11 @@
     down_d, up_d = {"dom": jnp.maximum(d - 1, 0)}, {"dom": jnp.minimum(d + 1, n_dom - 1)}
     down_s, up_s = {"sub": jnp.maximum(s - 1, 0)}, {"sub": jnp.minimum(s + 1, n_sub - 1)}
 
-    def strip_copies(source, target, send, recv, devices):
+    def strip_copies(source, target, first, send, recv, devices):
         return [
             pltpu.make_async_remote_copy(
                 src_ref=source.at[pl.ds(b * strip, strip)],
-                dst_ref=target.at[pl.ds(b * strip, strip)],
+                dst_ref=target.at[pl.ds(first + b * strip, strip)],
                 send_sem=send.at[b],
                 recv_sem=recv.at[b],
                 device_id=devices[b],
@@ -275,7 +273,7 @@
         for condition, action in zip(conditions, actions):
             pl.when(condition)(action)
 
-    h_copies = strip_copies(strips, halo, h_send, h_recv, (down_d, up_d, down_s, up_s))
+    h_copies = strip_copies(strips, table, n_own, h_send, h_recv, (down_d, up_d, down_s, up_s))
     h_to, h_from = (low_d, high_d, low_s, high_s), (high_d, low_d, high_s, low_s)
     when_all(h_to, [c.start for c in h_copies])
 
@@ -285,7 +283,7 @@
     step = 256 if edges % 256 == 0 else LANES
 
     def indices(cut_e, at, carry):
-        line = pl.ds(at // LANES, 1)
+        line = slice(at // LANES, at // LANES + 1)
         dst = dst_ref[line, :]
         direction = dir_ref[line, :]
         row = jnp.floor((dst.astype(F32) + 0.5) * (1.0 / side)).astype(jnp.int32)
@@ -319,22 +317,18 @@
     each_chunk(edges, LANES, indices)
     x_e[:, 0:lat] = feat_ref[...]
 
-    def gather(cut, at, carry):
-        x_e[cut, 2 * lat :] = mm(s_dst[cut, :], own[...]).astype(BF)
-        x_e[cut, lat : 2 * lat] = mm(s_src[cut, 0:n_own], own[...]).astype(BF)
+    def gather_dst(cut, at, carry):
+        x_e[cut, 2 * lat :] = mm(s_dst[cut, :], table[0:n_own, :]).astype(BF)
         return carry
 
-    each_chunk(edges, step, gather)
-
+    each_chunk(edges, step, gather_dst)
     when_all(h_from, [c.wait_recv for c in h_copies])
 
-    def gather_far(cut, at, carry):
-        far = mm(s_src[cut, n_own:], halo[...])
-        near = x_e[cut, lat : 2 * lat].astype(F32)
-        x_e[cut, lat : 2 * lat] = (near + far).astype(BF)
+    def gather_src(cut, at, carry):
+        x_e[cut, lat : 2 * lat] = mm(s_src[cut, :], table[...]).astype(BF)
         return carry
 
-    each_chunk(edges, step, gather_far)
+    each_chunk(edges, step, gather_src)
     for copy in w_copies:
         copy.wait_recv()
 
@@ -369,7 +363,7 @@
     for load in loads[9:]:
         load.wait()
     scale = (n_dom * n_sub * nodes) ** -0.5
-    x_n[:, 0:lat] = own[...]
+    x_n[:, 0:lat] = table[0:n_own, :]
     x_n[:, lat:] = agg[...]
 
     def node_both(cut, at, gain_sum):
@@ -416,7 +410,7 @@
             copies.append(copy)
         return copies
 
-    pack("node_in", mm_tn(x_n[0:nodes, :], gpre_n[...]))
+    pack("node_in", mm_tn(gpre_n[...], x_n[0:nodes, :]).T)
     pack("node_out", mm_tn(hid_n[...], graw_n[...]))
     n_copies = dom_copies(0, plan.node_part, n_send, n_recv)
 
@@ -432,7 +426,7 @@
 
     edge_gain = each_chunk(edges, step, edge_backward, jnp.zeros((1, lat), F32))
 
-    pack("edge_in", mm_tn(x_e[...], gpre_e[...]))
+    pack("edge_in", mm_tn(gpre_e[...], x_e[...]).T)
     pack("edge_out", mm_tn(hid_e[...], graw_e[...]))
     row16 = iota((16, lat), 0)
     gains16 = jnp.where(row16 == 0, edge_gain, jnp.where(row16 == 1, node_gain, 0.0))
@@ -445,7 +439,7 @@
     w_src, w_dst = w1e[lat : 2 * lat, :], w1e[2 * lat :, :]
     back = mm(t_src[n_own:, :], gpre_e[...]).astype(BF)
     gstrips[...] = mm_nt(back, w_src).astype(BF)
-    b_copies = strip_copies(gstrips, ghalo, b_send, b_recv, (up_d, down_d, up_s, down_s))
+    b_copies = strip_copies(gstrips, ghalo, 0, b_send, b_recv, (up_d, down_d, up_s, down_s))
     when_all(h_from, [c.start for c in b_copies])
 
 
@@ -607,8 +601,7 @@
             pltpu.VMEM((edges, lat), BF),
             dma((11,)),
             pltpu.VMEM((n_dom, plan.shard, lat), BF),
-            pltpu.VMEM((n_own, lat), BF),
-            pltpu.VMEM((n_halo, lat), BF),
+            pltpu.VMEM((table, lat), BF),
             pltpu.VMEM((n_halo, lat), BF),
             pltpu.VMEM((n_halo, lat), BF),
             pltpu.VMEM((n_halo, lat), BF),

time: 35.2 us -> 32.1 us (0.912)
  Pallas kernels: 33.7 us -> 30.7 us
    pallas_call x1, Pallas kernels: 31.9 us -> 28.8 us  [shards(): pl.pallas_call(functools.partial(kernel, plan), out_shape=out_shape, in_s...]
where the time goes in v4:
time: 32.1 us; the launch traced here: 32 us
  Pallas kernels  30.7 us (96%)
  between operations  1.29 us (4%)
    pallas_call x1, Pallas kernels, shards(): pl.pallas_call(functools.partial(kernel, plan), out_shape=out_shape, in_s...  28.8 us
    pallas_call x1, Pallas kernels, shards(): pl.pallas_call(write_out, out_shape=out_shape, in_specs=[hbm] * 7, out_sp...  1.88 us

profile of v4, /device:TPU:0, one launch (start us, length us, event | category | flops | bytes accessed | tf_op | source)
XLA Modules:
  0.0 32.0 jit_solution(16402714536405909289)
XLA Ops:
  1.3 28.8 %graph_layer_backward.1 = (bf16[576,128]{1,0:T(8,128)(2,1)}, bf16[1024,128]{1,0:T(8,128)(2,1)}, f32[96,128]{1,0:T(8,128)}, f32[32,128]{1,0:T(8,128)}, f32[64,128...) custom-call(bf16[576,128]{1,0:T(8,128)(2,1)} %bitcast.5, bf16[1024,128]{1,0:T(8,128)(2,1)} %feat_hbm.1, ...), custom_call_target="tpu_custom_call" | custom-call | tf_op jit(solution)/shard_map/graph_layer_backward/pallas_call | solution.py:583
  30.1 1.9 %write_results.1 = (bf16[576,128]{1,0:T(8,128)(2,1)}, bf16[1024,128]{1,0:T(8,128)(2,1)}, f32[96,128]{1,0:T(8,128)}, f32[32,128]{1,0:T(8,128)}, f32[64,128]{1,0:T...) custom-call(bf16[576,128]{1,0:T(8,128)(2,1)} %get-tuple-element.21.refs_0_, bf16[1024,128]{1,0:T(8,128)(2,1)} %get-tuple-element.22.refs_1_, ...), custom_call_target="tpu_custom_call" | custom-call | tf_op jit(solution)/shard_map/write_results/pallas_call | solution.py:663

commit v5 on v4

--- a/solution.py
+++ b/solution.py
@@ -149,6 +149,8 @@
     fin,
     w_send,
     w_recv,
+    v_send,
+    v_recv,
     h_send,
     h_recv,
     b_send,
@@ -238,18 +240,22 @@
 
     pl.semaphore_wait(barrier, (n_dom - 1) + (n_sub - 1))
 
-    w_copies = []
-    for k in range(1, n_dom):
-        copy = pltpu.make_async_remote_copy(
-            src_ref=wbuf.at[d],
-            dst_ref=wbuf.at[d],
-            send_sem=w_send.at[k],
-            recv_sem=w_recv.at[k],
-            device_id={"dom": lax.rem(d + k, n_dom)},
-            device_id_type=MESH,
-        )
-        copy.start()
-        w_copies.append(copy)
+    def weight_copies(first, last, send, recv):
+        copies = []
+        for k in range(1, n_dom):
+            copy = pltpu.make_async_remote_copy(
+                src_ref=wbuf.at[d, pl.ds(first, last - first)],
+                dst_ref=wbuf.at[d, pl.ds(first, last - first)],
+                send_sem=send.at[k],
+                recv_sem=recv.at[k],
+                device_id={"dom": lax.rem(d + k, n_dom)},
+                device_id_type=MESH,
+            )
+            copy.start()
+            copies.append(copy)
+        return copies
+
+    w_copies = weight_copies(plan.node_part, plan.shard, w_send, w_recv)
 
     low_d, high_d = d > 0, d < n_dom - 1
     low_s, high_s = s > 0, s < n_sub - 1
@@ -276,11 +282,12 @@
     h_copies = strip_copies(strips, table, n_own, h_send, h_recv, (down_d, up_d, down_s, up_s))
     h_to, h_from = (low_d, high_d, low_s, high_s), (high_d, low_d, high_s, low_s)
     when_all(h_to, [c.start for c in h_copies])
+    v_copies = weight_copies(0, plan.node_part, v_send, v_recv)
 
     for load in loads[6:9]:
         load.wait()
     count = count_ref[0]
-    step = 256 if edges % 256 == 0 else LANES
+    step = max(n for n in (128, 256, 512) if edges % n == 0)
 
     def indices(cut_e, at, carry):
         line = slice(at // LANES, at // LANES + 1)
@@ -340,7 +347,7 @@
         parts = [wbuf[n, at : at + padded, :].astype(F32)[0:size, :] for n in range(n_dom)]
         return jnp.concatenate(parts, axis=0).astype(BF)
 
-    w1e, w2e, w1n, w2n = whole("edge_in"), whole("edge_out"), whole("node_in"), whole("node_out")
+    w1e, w2e = whole("edge_in"), whole("edge_out")
     gains = sum(wbuf[n, off["gains"] : off["gains"] + 16, :].astype(F32) for n in range(n_dom))
     gain_edge, gain_node = gains[0:1, :], gains[1:2, :]
 
@@ -363,6 +370,9 @@
     for load in loads[9:]:
         load.wait()
     scale = (n_dom * n_sub * nodes) ** -0.5
+    for copy in v_copies:
+        copy.wait_recv()
+    w1n, w2n = whole("node_in"), whole("node_out")
     x_n[:, 0:lat] = table[0:n_own, :]
     x_n[:, lat:] = agg[...]
 
@@ -381,7 +391,7 @@
         agg[cut, :] = grad_in[:, lat:].astype(BF)
         return gain_sum + jnp.sum(upstream * normed, axis=0, keepdims=True)
 
-    node_step = max(n for n in range(16, 193, 16) if nodes % n == 0)
+    node_step = max(n for n in range(16, 289, 16) if nodes % n == 0)
     node_gain = each_chunk(nodes, node_step, node_both, jnp.zeros((1, lat), F32))
 
     def pack(name, value):
@@ -450,10 +460,6 @@
 
     each_chunk(edges, step, edge_result)
     stores[1].start()
-
-    at_src = mm(t_src[0:n_own, :], gpre_e[...]).astype(BF)
-    at_dst = mm(t_dst[...], gpre_e[...]).astype(BF)
-    spread = mm_nt(at_src, w_src) + mm_nt(at_dst, w_dst)
 
     for copy in n_copies + e_copies:
         copy.wait_recv()
@@ -475,17 +481,9 @@
         copy.start()
         q_copies.append(copy)
 
-    when_all(h_to, [c.wait_recv for c in b_copies])
-    pos = iota((n_own, n_halo), 1)
-    node_id = iota((n_own, n_halo), 0)
-    picked = jnp.zeros((n_own, n_halo), jnp.bool_)
-    for b in range(4):
-        at = pos - b * strip
-        border = (at, (side - 1) * side + at, at * side, at * side + side - 1)[b]
-        picked = picked | ((at >= 0) & (at < side) & (node_id == border))
-    spread = spread + mm(one_hot(picked), ghalo[...])
-    node_out[...] = (node_acc[...] + spread[0:nodes, :]).astype(BF)
-    stores[0].start()
+    at_src = mm(t_src[0:n_own, :], gpre_e[...]).astype(BF)
+    at_dst = mm(t_dst[...], gpre_e[...]).astype(BF)
+    spread = mm_nt(at_src, w_src) + mm_nt(at_dst, w_dst)
 
     for copy in q_copies:
         copy.wait_recv()
@@ -505,6 +503,18 @@
         )
         copy.start()
         f_copies.append(copy)
+    when_all(h_to, [c.wait_recv for c in b_copies])
+    pos = iota((n_own, n_halo), 1)
+    node_id = iota((n_own, n_halo), 0)
+    picked = jnp.zeros((n_own, n_halo), jnp.bool_)
+    for b in range(4):
+        at = pos - b * strip
+        border = (at, (side - 1) * side + at, at * side, at * side + side - 1)[b]
+        picked = picked | ((at >= 0) & (at < side) & (node_id == border))
+    spread = spread + mm(one_hot(picked), ghalo[...])
+    node_out[...] = (node_acc[...] + spread[0:nodes, :]).astype(BF)
+    stores[0].start()
+
     for copy in f_copies:
         copy.wait_recv()
     result = fin[...].reshape(plan.total, lat)
@@ -521,7 +531,7 @@
     for store in stores[2:]:
         store.start()
 
-    for copy in w_copies + n_copies + e_copies + q_copies + f_copies:
+    for copy in w_copies + v_copies + n_copies + e_copies + q_copies + f_copies:
         copy.wait_send()
     when_all(h_to, [c.wait_send for c in h_copies])
     when_all(h_from, [c.wait_send for c in b_copies])
@@ -629,6 +639,8 @@
             pltpu.VMEM((n_sub, plan.piece, lat), BF),
             dma((n_dom,)),
             dma((n_dom,)),
+            dma((n_dom,)),
+            dma((n_dom,)),
             dma((4,)),
             dma((4,)),
             dma((4,)),

time: 32.1 us -> 30.9 us (0.963)
  Pallas kernels: 30.7 us -> 29.4 us
    pallas_call x1, Pallas kernels: 28.8 us -> 27.5 us  [shards(): pl.pallas_call(functools.partial(kernel, plan), out_shape=out_shape, in_s...]
where the time goes in v5:
time: 30.9 us; the launch traced here: 30.7 us
  Pallas kernels  29.4 us (95%)
  between operations  1.29 us (4%)
    pallas_call x1, Pallas kernels, shards(): pl.pallas_call(functools.partial(kernel, plan), out_shape=out_shape, in_s...  27.5 us
    pallas_call x1, Pallas kernels, shards(): pl.pallas_call(write_out, out_shape=out_shape, in_specs=[hbm] * 7, out_sp...  1.88 us

profile of v5, /device:TPU:0, one launch (start us, length us, event | category | flops | bytes accessed | tf_op | source)
XLA Modules:
  0.0 30.7 jit_solution(4760947429306630150)
XLA Ops:
  1.3 27.5 %graph_layer_backward.1 = (bf16[576,128]{1,0:T(8,128)(2,1)}, bf16[1024,128]{1,0:T(8,128)(2,1)}, f32[96,128]{1,0:T(8,128)}, f32[32,128]{1,0:T(8,128)}, f32[64,128...) custom-call(bf16[576,128]{1,0:T(8,128)(2,1)} %bitcast.5, bf16[1024,128]{1,0:T(8,128)(2,1)} %feat_hbm.1, ...), custom_call_target="tpu_custom_call" | custom-call | tf_op jit(solution)/shard_map/graph_layer_backward/pallas_call | solution.py:593
  28.8 1.9 %write_results.1 = (bf16[576,128]{1,0:T(8,128)(2,1)}, bf16[1024,128]{1,0:T(8,128)(2,1)}, f32[96,128]{1,0:T(8,128)}, f32[32,128]{1,0:T(8,128)}, f32[64,128]{1,0:T...) custom-call(bf16[576,128]{1,0:T(8,128)(2,1)} %get-tuple-element.21.refs_0_, bf16[1024,128]{1,0:T(8,128)(2,1)} %get-tuple-element.22.refs_1_, ...), custom_call_target="tpu_custom_call" | custom-call | tf_op jit(solution)/shard_map/write_results/pallas_call | solution.py:675

commit v6 on v5

--- a/solution.py
+++ b/solution.py
@@ -287,7 +287,7 @@
     for load in loads[6:9]:
         load.wait()
     count = count_ref[0]
-    step = max(n for n in (128, 256, 512) if edges % n == 0)
+    step = max(n for n in (128, 256, 512, 1024) if edges % n == 0)
 
     def indices(cut_e, at, carry):
         line = slice(at // LANES, at // LANES + 1)
@@ -391,7 +391,7 @@
         agg[cut, :] = grad_in[:, lat:].astype(BF)
         return gain_sum + jnp.sum(upstream * normed, axis=0, keepdims=True)
 
-    node_step = max(n for n in range(16, 289, 16) if nodes % n == 0)
+    node_step = max(n for n in range(16, 577, 16) if nodes % n == 0)
     node_gain = each_chunk(nodes, node_step, node_both, jnp.zeros((1, lat), F32))
 
     def pack(name, value):

time: 30.9 us -> 31 us (level)
  no operation moved by 1% of the time
where the time goes in v6:
time: 31 us; the launch traced here: 30.8 us
  Pallas kernels  29.5 us (95%)
  between operations  1.29 us (4%)
    pallas_call x1, Pallas kernels, shards(): pl.pallas_call(functools.partial(kernel, plan), out_shape=out_shape, in_s...  27.7 us
    pallas_call x1, Pallas kernels, shards(): pl.pallas_call(write_out, out_shape=out_shape, in_specs=[hbm] * 7, out_sp...  1.88 us

profile of v6, /device:TPU:0, one launch (start us, length us, event | category | flops | bytes accessed | tf_op | source)
XLA Modules:
  0.0 30.8 jit_solution(17042761171943575470)
XLA Ops:
  1.3 27.7 %graph_layer_backward.1 = (bf16[576,128]{1,0:T(8,128)(2,1)}, bf16[1024,128]{1,0:T(8,128)(2,1)}, f32[96,128]{1,0:T(8,128)}, f32[32,128]{1,0:T(8,128)}, f32[64,128...) custom-call(bf16[576,128]{1,0:T(8,128)(2,1)} %bitcast.5, bf16[1024,128]{1,0:T(8,128)(2,1)} %feat_hbm.1, ...), custom_call_target="tpu_custom_call" | custom-call | tf_op jit(solution)/shard_map/graph_layer_backward/pallas_call | solution.py:593
  28.9 1.9 %write_results.1 = (bf16[576,128]{1,0:T(8,128)(2,1)}, bf16[1024,128]{1,0:T(8,128)(2,1)}, f32[96,128]{1,0:T(8,128)}, f32[32,128]{1,0:T(8,128)}, f32[64,128]{1,0:T...) custom-call(bf16[576,128]{1,0:T(8,128)(2,1)} %get-tuple-element.21.refs_0_, bf16[1024,128]{1,0:T(8,128)(2,1)} %get-tuple-element.22.refs_1_, ...), custom_call_target="tpu_custom_call" | custom-call | tf_op jit(solution)/shard_map/write_results/pallas_call | solution.py:675
